TPU v7x, 128 devices: a whole 4x4x4 slice. The times are simulated.
128 devices in a mesh: dp: 8 (over y, core), fsdp: 16 (over z, x).
Axes of the slice: x: 4, y: 4, z: 4, core: 2. Of those that a mesh axis runs over, the one named last changes fastest.
Arguments:
- old_shards: bfloat16 [8, 16, 38230, 128], P('dp', 'fsdp'), may hold values from -0.0625 to 0.0625
- shard_table: int32 [96, 4], replicated, may hold values from 0 to 917501, as said below
- tokens: bfloat16 [2048, 8192], P('dp', 'fsdp'), may hold values from -6 to 6
- cotangent: bfloat16 [2048, 14336], P('fsdp', 'dp'), may hold values from -0.125 to 0.125
Outputs:
- grad_gate: bfloat16 [8192, 14336], P('fsdp', 'dp')
- grad_up: bfloat16 [8192, 14336], P('fsdp', 'dp')
Inputs may be any that keep to these rules, and one draw needn't show every extreme that they name: `shard_table`: rows run over matrix m, then row block f of 57344 128-value rows, then j < 3; shard (m, f, j) begins within block f, is held by device (dp m * 3 + j, fsdp f), and ends where the next shard of its matrix begins (the last at 917504); the first shard of each matrix begins at 0, and the last shard of the up projection begins at 8192 * 112 - 57344 % 3 - 1. Lengths run from 1 to 38229, and that largest length is reached in every draw.
All inputs are finite; a program needn't handle non-finite values.
Results may differ from a plain program's by a relative error of at most 0.023.
Values may be sent and summed in bfloat16 or wider, within the bound.
No kernel may reach another device: no remote copies, remote signals or barrier semaphores. Data moves between devices by JAX's collectives and lax.ppermute only.
A program may use at most 192 MiB of HBM per device.

v0:
```python
import jax
import jax.numpy as jnp
from jax import lax
from jax.sharding import PartitionSpec as P


def from_behind(value, axis, steps):
    count = lax.axis_size(axis)
    leading, last = (max(0, -steps), min(count, count - steps))
    return lax.ppermute(value, axis, [(source, source + steps) for source in range(leading, last)])


def swiglu_backward(summed, upstream, hidden):
    gate = summed[:, :hidden]
    upper = summed[:, hidden:]
    incoming = upstream.astype(jnp.float32)
    sigma = jax.nn.sigmoid(gate)
    grad_gate = incoming * upper * sigma * (1.0 + gate * (1.0 - sigma))
    grad_upper = incoming * gate * sigma
    return jnp.concatenate([grad_gate, grad_upper], axis=1).astype(jnp.bfloat16)


def on_device(old_shards, shard_table, tokens, cotangent):
    n_data = lax.axis_size("dp")
    n_feature = lax.axis_size("fsdp")
    data_index = lax.axis_index("dp")
    feature_index = lax.axis_index("fsdp")
    block_rows = tokens.shape[1]
    hidden = cotangent.shape[1]
    col_units = hidden // 128
    row_units = col_units * n_data
    capacity = old_shards.shape[2]
    slot_rows = capacity // row_units + 2
    per_block = 3 * n_data // 8
    shard_total = shard_table.shape[0]
    zero_index = jnp.zeros((), jnp.int32)
    matrix_id = data_index // per_block
    within = data_index % per_block
    holder = data_index < 2 * per_block
    table_row = jnp.minimum(
        (matrix_id * n_feature + feature_index) * per_block + within, shard_total - 1
    )
    my_entry = lax.dynamic_index_in_dim(shard_table, table_row, 0, keepdims=False)
    first_unit = my_entry[0]
    unit_count = my_entry[1]
    live = (jnp.arange(capacity, dtype=jnp.int32) < unit_count) & holder
    payload = jnp.where(live[:, None], old_shards[0, 0], jnp.zeros((), jnp.bfloat16))
    lead_units = first_unit % row_units
    padded = jnp.zeros((slot_rows * row_units, 128), jnp.bfloat16)
    padded = lax.dynamic_update_slice(padded, payload, (lead_units, zero_index))
    outgoing = padded.reshape(slot_rows, n_data, col_units, 128).transpose(1, 0, 2, 3)
    incoming = lax.all_to_all(outgoing, "dp", split_axis=0, concat_axis=0, tiled=True)
    extended = jnp.zeros((2, block_rows + slot_rows, col_units, 128), jnp.bfloat16)
    for source in range(2 * per_block):
        source_matrix = source // per_block
        entry_row = (source_matrix * n_feature + feature_index) * per_block + source % per_block
        source_first = lax.dynamic_index_in_dim(shard_table, entry_row, 0, keepdims=False)[0]
        row_offset = source_first // row_units - feature_index * block_rows
        layer_slab = extended[source_matrix]
        current = lax.dynamic_slice(
            layer_slab, (row_offset, zero_index, zero_index), (slot_rows, col_units, 128)
        )
        layer_slab = lax.dynamic_update_slice(
            layer_slab, current + incoming[source], (row_offset, zero_index, zero_index)
        )
        extended = extended.at[source_matrix].set(layer_slab)
    spill_count = min(block_rows, slot_rows)
    carried = from_behind(extended[:, block_rows : block_rows + spill_count], "fsdp", 1)
    owned = extended[:, :block_rows].at[:, :spill_count].add(carried)
    joined = owned.transpose(1, 0, 2, 3).reshape(block_rows, 2 * hidden)
    all_rows = lax.all_gather(tokens, "dp", axis=0, tiled=True)
    partial_term = jnp.dot(all_rows, joined, preferred_element_type=jnp.float32)
    summed = lax.psum(partial_term.astype(jnp.bfloat16), "fsdp").astype(jnp.float32)
    upstream = lax.all_gather(cotangent, "fsdp", axis=0, tiled=True)
    grads_in = swiglu_backward(summed, upstream, hidden)
    total = lax.dot_general(
        all_rows, grads_in, (((0,), (0,)), ((), ())), preferred_element_type=jnp.float32
    )
    return (total[:, :hidden].astype(jnp.bfloat16), total[:, hidden:].astype(jnp.bfloat16))


def solution(mesh):
    return jax.shard_map(
        on_device,
        mesh=mesh,
        in_specs=(P("dp", "fsdp", None, None), P(), P("dp", "fsdp"), P("fsdp", "dp")),
        out_specs=(P("fsdp", "dp"), P("fsdp", "dp")),
        check_vma=False,
    )
```

profile of v0, /device:TPU:1, one launch (start us, length us, event | category | flops | bytes accessed | tf_op | source)
XLA Modules:
  0.0 784.8 jit_solution(9589543788057127880)
XLA Ops:
  10.1 21.9 %bitcast_select_fusion = bf16[38230,128]{1,0:T(8,128)(2,1)} fusion(bf16[1,1,38230,128]{3,2,1,0:T(8,128)(2,1)} %param.18, pred[38230]{0:T(1024)(128)(4,1)S(1)} %fusion.16), kind=kLoop, calls=%fused_computation.14 | loop fusion | flops 4893440 | bytes 19611990 | tf_op jit(solution)/shard_map/jit(_where)/select_n | solution.py:47
  32.0 4.7 broadcast_in_dim.17
  36.6 44.8 %dynamic_update_slice.39 = bf16[38416,128]{1,0:T(8,128)(2,1)} dynamic-update-slice(bf16[38416,128]{1,0:T(8,128)(2,1)} %broadcast_in_dim.17, bf16[38230,128]{1,0:T(8,128)(2,1)} %bitcast_select_fusion, s32[]{:T(128)S(6)} %select_n.90, s32[]{:T(128)} %constant.289.clone.1) | dynamic-update-slice | bytes 19573764 | tf_op jit(solution)/shard_map/dynamic_update_slice | solution.py:50
  81.5 15.5 %reshape.370 = bf16[343,8,14,128]{3,2,1,0:T(8,128)(2,1)} reshape(bf16[38416,128]{1,0:T(8,128)(2,1)} %dynamic_update_slice.39) | data formatting | bytes 19668992 | tf_op jit(solution)/shard_map/reshape | solution.py:51
  97.0 14.2 %copy.14 = bf16[8,343,14,128]{3,1,2,0:T(8,128)(2,1)} copy(bf16[8,343,14,128]{3,2,0,1:T(8,128)(2,1)} %bitcast.27) | data formatting | bytes 19668992 | tf_op jit(solution)/shard_map/transpose | solution.py:51
  111.1 6.6 all-to-all-start
  133.4 102.4 %all-to-all-done = bf16[8,343,14,128]{3,1,2,0:T(8,128)(2,1)} async-done(((bf16[8,343,14,128]{3,1,2,0:T(8,128)(2,1)}), bf16[8,343,14,128]{3,1,2,0:T(8,128)(2,1)}, u32[]{:S(2)}, u32[]{:S(2)}) %all-to-all-start) | async-done | bytes 9834528 | tf_op jit(solution)/shard_map/all_to_all | solution.py:52
  235.8 5.5 fusion.18
  241.4 2.9 copy.30
  255.3 10.1 %dynamic_update_slice.40 = bf16[1,855,14,128]{1,3,2,0:T(8,128)(2,1)S(1)} dynamic-update-slice(bf16[1,855,14,128]{1,3,2,0:T(8,128)(2,1)S(1)} %squeeze.14, bf16[1,343,14,128]{1,3,2,0:T(8,128)(2,1)} %copy.25, s32[]{:T(128)} %constant.289.clone.1, s32[]{:T(128)S(6)} %select_n.93, s32[]{:T(128)} %constant.289.clone.1, s32[]{:T(128)} %constant.289.clone.1) | dynamic-update-slice | bytes 2458628 | tf_op jit(solution)/shard_map/dynamic_update_slice | solution.py:63
  265.4 3.6 scatter.20
  270.9 12.2 %dynamic_update_slice.41 = bf16[1,855,14,128]{1,3,2,0:T(8,128)(2,1)S(1)} dynamic-update-slice(bf16[1,855,14,128]{1,3,2,0:T(8,128)(2,1)S(1)} %dynamic_update_slice.40, bf16[1,343,14,128]{1,3,2,0:T(8,128)(2,1)} %dynamic-slice_add_fusion.4, s32[]{:T(128)} %constant.289.clone.1, s32[]{:T(128)S(6)} %select_n.96, s32[]{:T(128)} %constant.289.clone.1, s32[]{:T(128)} %constant.289.clone.1) | dynamic-update-slice | bytes 2458628 | tf_op jit(solution)/shard_map/dynamic_update_slice | solution.py:63
  287.1 12.1 %dynamic_update_slice.42 = bf16[1,855,14,128]{1,3,2,0:T(8,128)(2,1)S(1)} dynamic-update-slice(bf16[1,855,14,128]{1,3,2,0:T(8,128)(2,1)S(1)} %dynamic_update_slice.41, bf16[1,343,14,128]{1,3,2,0:T(8,128)(2,1)} %dynamic-slice_add_fusion.3, s32[]{:T(128)} %constant.289.clone.1, s32[]{:T(128)S(6)} %select_n.99, s32[]{:T(128)} %constant.289.clone.1, s32[]{:T(128)} %constant.289.clone.1) | dynamic-update-slice | bytes 2458628 | tf_op jit(solution)/shard_map/dynamic_update_slice | solution.py:63
  305.6 10.0 %dynamic_update_slice.43 = bf16[1,855,14,128]{1,3,2,0:T(8,128)(2,1)S(1)} dynamic-update-slice(bf16[1,855,14,128]{1,3,2,0:T(8,128)(2,1)S(1)} %slice.281, bf16[1,343,14,128]{1,3,2,0:T(8,128)(2,1)} %dynamic-slice_add_fusion.2, s32[]{:T(128)} %constant.289.clone.1, s32[]{:T(128)S(6)} %select_n.102, s32[]{:T(128)} %constant.289.clone.1, s32[]{:T(128)} %constant.289.clone.1) | dynamic-update-slice | bytes 2458628 | tf_op jit(solution)/shard_map/dynamic_update_slice | solution.py:63
  315.6 3.3 dynamic-slice_add_fusion.1
  320.9 12.2 %dynamic_update_slice.44 = bf16[1,855,14,128]{1,3,2,0:T(8,128)(2,1)S(1)} dynamic-update-slice(bf16[1,855,14,128]{1,3,2,0:T(8,128)(2,1)S(1)} %dynamic_update_slice.43, bf16[1,343,14,128]{1,3,2,0:T(8,128)(2,1)} %dynamic-slice_add_fusion.1, s32[]{:T(128)} %constant.289.clone.1, s32[]{:T(128)S(6)} %select_n.105, s32[]{:T(128)} %constant.289.clone.1, s32[]{:T(128)} %constant.289.clone.1) | dynamic-update-slice | bytes 2458628 | tf_op jit(solution)/shard_map/dynamic_update_slice | solution.py:63
  337.2 12.2 %dynamic_update_slice.45 = bf16[1,855,14,128]{1,3,2,0:T(8,128)(2,1)S(1)} dynamic-update-slice(bf16[1,855,14,128]{1,3,2,0:T(8,128)(2,1)S(1)} %dynamic_update_slice.44, bf16[1,343,14,128]{1,3,2,0:T(8,128)(2,1)} %dynamic-slice_add_fusion, s32[]{:T(128)} %constant.289.clone.1, s32[]{:T(128)S(6)} %select_n.108, s32[]{:T(128)} %constant.289.clone.1, s32[]{:T(128)} %constant.289.clone.1) | dynamic-update-slice | bytes 2458628 | tf_op jit(solution)/shard_map/dynamic_update_slice | solution.py:63
  353.5 5.9 copy.21
  359.4 7.3 collective-permute-start
  366.7 4.2 slice.285
  370.9 47.7 %collective-permute-done = bf16[2,343,14,128]{3,0,2,1:T(2,128)(2,1)S(1)} collective-permute-done((bf16[2,343,14,128]{3,0,2,1:T(2,128)(2,1)}, bf16[2,343,14,128]{3,0,2,1:T(2,128)(2,1)S(1)}, u32[]{:S(2)}, u32[]{:S(2)}) %collective-permute-start) | collective-permute-done | bytes 2458656 | tf_op jit(solution)/shard_map/ppermute | solution.py:10
  418.7 6.2 copy.22
  424.9 2.9 slice_add_fusion
  427.8 17.5 %scatter-add.4 = bf16[2,512,14,128]{1,3,2,0:T(8,128)(2,1)} dynamic-update-slice(bf16[2,512,14,128]{1,3,2,0:T(8,128)(2,1)} %slice.285, bf16[2,343,14,128]{1,3,2,0:T(8,128)(2,1)S(1)} %slice_add_fusion, s32[]{:T(128)} %constant.289.clone.1, s32[]{:T(128)} %constant.289.clone.1, s32[]{:T(128)} %constant.289.clone.1, s32[]{:T(128)} %constant.289.clone.1) | dynamic-update-slice | bytes 4917252 | tf_op jit(solution)/shard_map/scatter-add | solution.py:69
  445.4 13.4 %fusion.9 = bf16[2048,3584]{0,1:T(8,128)(2,1)} fusion(bf16[512,3584]{0,1:T(8,128)(2,1)} %bitcast.28, bf16[2048,512]{1,0:T(8,128)(2,1)} %all-gather.5.cloned.1.call-done), kind=kOutput, calls=%fused_computation.13 | convolution fusion | flops 7523532800 | bytes 20447232 | tf_op jit(solution)/shard_map/dot_general | solution.py:72
  460.8 199.8 %all-reduce.3.cloned.1.call-done = bf16[2048,3584]{0,1:T(8,128)(2,1)} async-done(((bf16[2048,3584]{0,1:T(8,128)(2,1)}), bf16[2048,3584]{0,1:T(8,128)(2,1)}) %all-reduce.3.cloned.1.call-update) | async-done | bytes 14680080 | tf_op jit(solution)/shard_map/psum | solution.py:73
  660.5 16.8 %convert_element_type.18 = f32[2048,3584]{0,1:T(8,128)} convert(bf16[2048,3584]{0,1:T(8,128)(2,1)} %all-reduce.3.cloned.1.call-done) | non-fusion elementwise | flops 7340032 | bytes 44040192 | tf_op jit(solution)/shard_map/convert_element_type | solution.py:73
  677.3 58.1 %all-gather.3.cloned.1.call-done = bf16[2048,1792]{0,1:T(8,128)(2,1)} async-done(((bf16[128,1792]{0,1:T(8,128)(2,1)}), bf16[2048,1792]{0,1:T(8,128)(2,1)}) %all-gather.3.cloned.1.call-update) | async-done | bytes 7340048 | tf_op jit(solution)/shard_map/all_gather | solution.py:74
  735.5 18.2 %fusion.2 = (bf16[2048,1792]{0,1:T(8,128)(2,1)}, bf16[2048,1792]{0,1:T(8,128)(2,1)}) fusion(bf16[2048,1792]{0,1:T(8,128)(2,1)} %all-gather.3.cloned.1.call-done, f32[2048,3584]{0,1:T(8,128)} %convert_element_type.18), kind=kLoop, calls=%fused_computation.5 | loop fusion | flops 51380224 | bytes 51380224 | tf_op jit(solution)/shard_map/convert.2
  753.6 14.7 %fusion.13 = bf16[512,3584]{0,1:T(8,128)(2,1)} fusion(bf16[2048,512]{1,0:T(8,128)(2,1)S(1)} %copy-done.5, bf16[2048,1792]{0,1:T(8,128)(2,1)} %get-tuple-element.93, bf16[2048,1792]{0,1:T(8,128)(2,1)} %get-tuple-element.92), kind=kOutput, calls=%fused_computation.16 | convolution fusion | flops 7547387904 | bytes 20447232 | tf_op jit(solution)/shard_map/dot_general | solution.py:76
  768.4 3.5 fusion.19
  771.9 3.8 copy.24
  (47 shorter events, 43.8 us)
Async XLA Ops:
  111.1 124.7 %all-to-all-start = ((bf16[8,343,14,128]{3,1,2,0:T(8,128)(2,1)}), bf16[8,343,14,128]{3,1,2,0:T(8,128)(2,1)}, u32[]{:S(2)}, u32[]{:S(2)}) async-start(bf16[8,343,14,128]{3,1,2,0:T(8,128)(2,1)} %copy.14), calls=%async_computation | async-start | bytes 19726336 | tf_op jit(solution)/shard_map/all_to_all | solution.py:52
  117.7 327.6 %all-gather.5.cloned.1.call-start = ((), (), s32[]{:S(2)}) async-start(), calls=%async_computation.2 | async-start | bytes 2359296 | tf_op jit(solution)/shard_map/all_gather | solution.py:71
  118.4 542.1 %all-reduce.3.cloned.1.call-start = ((), (), s32[]{:S(2)}) async-start(), calls=%async_computation.3 | async-start | bytes 29360128 | tf_op jit(solution)/shard_map/psum | solution.py:73
  265.4 3.6 copy-start.3
  283.1 2.0 copy-start.2
  301.3 2.4 copy-start.1
  333.1 2.1 copy-start
  359.4 59.3 %collective-permute-start = (bf16[2,343,14,128]{3,0,2,1:T(2,128)(2,1)}, bf16[2,343,14,128]{3,0,2,1:T(2,128)(2,1)S(1)}, u32[]{:S(2)}, u32[]{:S(2)}) collective-permute-start(bf16[2,343,14,128]{3,0,2,1:T(2,128)(2,1)} %copy.21), channel_id=1, source_target_pairs={{0,1},{1,2},{2,3},{3,4},{4,5},{5,6},{6,7},{7,8},{8,9},{9,10},{10,1... | collective-permute-start | bytes 7375880 | tf_op jit(solution)/shard_map/ppermute | solution.py:10
  458.7 1.0 copy-start.4
  458.8 276.7 %all-gather.3.cloned.1.call-start = ((), (), s32[]{:S(2)}) async-start(), calls=%async_computation.1 | async-start | bytes 7798784 | tf_op jit(solution)/shard_map/all_gather | solution.py:74
  677.3 76.3 %copy-start.5 = (bf16[2048,512]{1,0:T(8,128)(2,1)S(1)}, bf16[2048,512]{1,0:T(8,128)(2,1)}, u32[]{:S(2)}) copy-start(bf16[2048,512]{1,0:T(8,128)(2,1)} %all-gather.5.cloned.1.call-done) | copy-start | bytes 6291460
Sparse Core Ops, SparseCore 0:
  120.3 40.3 all-gather.4
  458.9 201.5 all-reduce.2
  663.4 71.9 all-gather.2
where the time goes:
time: 796 us; the launch traced here: 785 us
  waiting for transfers between devices  409 us (51%)
  local copies, waits for them, and re-layouts  236 us (30%)
  other arithmetic  71.5 us (9%)
  matrix products  28.1 us (4%)
  between operations  26.7 us (3%)
  starting transfers between devices  14 us (2%)
    psum x1, waiting for transfers between devices, on_device(): lax.psum(partial_term.astype(jnp.bfloat16), 'fsdp').astype(jnp.float32)  200 us
    all_to_all x1, waiting for transfers between devices, on_device(): lax.all_to_all(outgoing, 'dp', split_axis=0, concat_axis=0, tiled=True)  102 us
    dynamic_update_slice x6, local copies, waits for them, and re-layouts, on_device(): lax.dynamic_update_slice(layer_slab, current + incoming[source], (row_off...  68.8 us
    all_gather x1, waiting for transfers between devices, on_device(): upstream = lax.all_gather(cotangent, 'fsdp', axis=0, tiled=True)  58.1 us
    ppermute x1, waiting for transfers between devices, from_behind(): lax.ppermute(value, axis, [(source, source + steps) for source in range(l...  47.7 us
    dynamic_update_slice x1, local copies, waits for them, and re-layouts, on_device(): padded = lax.dynamic_update_slice(padded, payload, (lead_units, zero_index))  44.8 us
    select_n x1, other arithmetic, on_device(): jnp.where(live[:, None], old_shards[0, 0], jnp.zeros((), jnp.bfloat16))  21.9 us
    unnamed x21, local copies, waits for them, and re-layouts  21.6 us
  transfers between devices with their start and end apart: 5, of which 4 were waited for; matrix products, arithmetic and copies ran while one was open for 22% of the time, Pallas kernels for 0%

commit v1 on v0

v1 whole, which is shorter than its diff:
```python
import functools

import jax
import jax.numpy as jnp
from jax import lax
from jax.experimental import pallas as pl
from jax.experimental.pallas import tpu as pltpu
from jax.sharding import PartitionSpec as P

LANES = 128
GROUP = 16
ALIGN = 8


def from_ahead(value, axis, steps):
    count = lax.axis_size(axis)
    return lax.ppermute(value, axis, [(source, source - steps) for source in range(steps, count)])


def pack_kernel(place_ref, shard_ref, out_ref, units, *, row_units):
    group = pl.program_id(0)
    lead = place_ref[0]
    length = place_ref[1]
    block = GROUP * row_units
    held = ALIGN * row_units
    n_owner, _, width = out_ref.shape
    owned = width // LANES

    @pl.when(group == 0)
    def _():
        units[:held] = jnp.zeros((held, LANES), jnp.float32)

    @pl.when(group > 0)
    def _():
        units[:held] = units[block : block + held]

    position = group * block + lax.broadcasted_iota(jnp.int32, (block, LANES), 0)
    fresh = shard_ref[...].astype(jnp.float32)
    units[held:] = jnp.where(position < length, fresh, 0.0)
    for column in range(row_units):
        owner, unit = divmod(column, owned)
        rows = units[pl.ds(held - lead + column, GROUP, stride=row_units), :]
        out_ref[owner, :, unit * LANES : (unit + 1) * LANES] = rows.astype(out_ref.dtype)


def pack(place, shard, n_owner, row_units, slab_rows):
    block = GROUP * row_units
    last = pl.cdiv(shard.shape[0], block) - 1
    width = row_units // n_owner * LANES
    return pl.pallas_call(
        functools.partial(pack_kernel, row_units=row_units),
        out_shape=jax.ShapeDtypeStruct((n_owner, slab_rows, width), shard.dtype),
        grid_spec=pltpu.PrefetchScalarGridSpec(
            num_scalar_prefetch=1,
            grid=(slab_rows // GROUP,),
            in_specs=[pl.BlockSpec((block, LANES), lambda g, _: (jnp.minimum(g, last), 0))],
            out_specs=pl.BlockSpec((n_owner, GROUP, width), lambda g, _: (0, g, 0)),
            scratch_shapes=[pltpu.VMEM((block + ALIGN * row_units, LANES), jnp.float32)],
        ),
        compiler_params=pltpu.CompilerParams(vmem_limit_bytes=32 * 1024 * 1024),
        cost_estimate=pl.CostEstimate(
            flops=0, bytes_accessed=4 * shard.size, transcendentals=0
        ),
    )(place, shard)


def unpack_kernel(offset_ref, slab_ref, out_ref, total, *, per_matrix):
    matrix = pl.program_id(0)
    slab_rows = slab_ref.shape[1]
    total[...] = jnp.zeros_like(total)
    for source in range(per_matrix):
        start = pl.multiple_of(offset_ref[matrix * per_matrix + source], ALIGN)
        rows = pl.ds(start, slab_rows)
        total[rows, :] += slab_ref[source].astype(jnp.float32)
    out_ref[...] = total[...].astype(out_ref.dtype)


def unpack(offsets, slabs, per_matrix, rows_out, chunk):
    _, slab_rows, width = slabs.shape
    chunks = width // chunk
    return pl.pallas_call(
        functools.partial(unpack_kernel, per_matrix=per_matrix),
        out_shape=jax.ShapeDtypeStruct((rows_out, 2 * width), slabs.dtype),
        grid_spec=pltpu.PrefetchScalarGridSpec(
            num_scalar_prefetch=1,
            grid=(2, chunks),
            in_specs=[pl.BlockSpec((per_matrix, slab_rows, chunk), lambda m, c, _: (m, 0, c))],
            out_specs=pl.BlockSpec((rows_out, chunk), lambda m, c, _: (0, m * chunks + c)),
            scratch_shapes=[pltpu.VMEM((rows_out, chunk), jnp.float32)],
        ),
        compiler_params=pltpu.CompilerParams(vmem_limit_bytes=32 * 1024 * 1024),
        cost_estimate=pl.CostEstimate(
            flops=0, bytes_accessed=4 * rows_out * width + 2 * slabs.size, transcendentals=0
        ),
    )(offsets, slabs)


def swiglu_backward(summed, upstream, hidden):
    gate = summed[:, :hidden]
    upper = summed[:, hidden:]
    incoming = upstream.astype(jnp.float32)
    sigma = jax.nn.sigmoid(gate)
    grad_gate = incoming * upper * sigma * (1.0 + gate * (1.0 - sigma))
    grad_upper = incoming * gate * sigma
    return jnp.concatenate([grad_gate, grad_upper], axis=1).astype(jnp.bfloat16)


def on_device(old_shards, shard_table, tokens, cotangent):
    n_data = lax.axis_size("dp")
    n_feature = lax.axis_size("fsdp")
    data_index = lax.axis_index("dp")
    feature_index = lax.axis_index("fsdp")
    block_rows = tokens.shape[1]
    hidden = cotangent.shape[1]
    row_units = hidden // LANES * n_data
    capacity = old_shards.shape[2]
    per_block = 3
    first_row = feature_index * block_rows
    slab_rows = pl.cdiv(ALIGN * row_units + capacity, GROUP * row_units) * GROUP
    extended_rows = block_rows + pl.cdiv(slab_rows, LANES) * LANES

    matrix_id = data_index // per_block
    holder = data_index < 2 * per_block
    table_row = (matrix_id * n_feature + feature_index) * per_block + data_index % per_block
    my_entry = lax.dynamic_index_in_dim(
        shard_table, jnp.minimum(table_row, shard_table.shape[0] - 1), 0, keepdims=False
    )
    lead = (my_entry[0] - first_row * row_units) % (ALIGN * row_units)
    place = jnp.stack([lead, jnp.where(holder, my_entry[1], 0)])
    outgoing = pack(place, old_shards[0, 0], n_data, row_units, slab_rows)
    incoming = lax.all_to_all(outgoing, "dp", split_axis=0, concat_axis=0, tiled=True)

    ahead = from_ahead(tokens[:, : extended_rows - block_rows], "fsdp", 1)
    widened = jnp.concatenate([tokens, ahead], axis=1)
    all_rows = lax.all_gather(widened, "dp", axis=0, tiled=True)

    firsts = shard_table[:, 0].reshape(2, n_feature, per_block)
    firsts = lax.dynamic_index_in_dim(firsts, feature_index, 1, keepdims=False).reshape(-1)
    offsets = (firsts // row_units - first_row) // ALIGN * ALIGN
    joined = unpack(offsets, incoming, per_block, extended_rows, 2 * LANES)

    partial_term = jnp.dot(all_rows, joined, preferred_element_type=jnp.float32)
    summed = lax.psum_scatter(
        partial_term.astype(jnp.bfloat16), "fsdp", scatter_dimension=0, tiled=True
    ).astype(jnp.float32)
    grads_own = swiglu_backward(summed, cotangent, hidden)
    grads_in = lax.all_gather(grads_own, "fsdp", axis=0, tiled=True)
    total = lax.dot_general(
        all_rows[:, :block_rows],
        grads_in,
        (((0,), (0,)), ((), ())),
        preferred_element_type=jnp.float32,
    )
    return (total[:, :hidden].astype(jnp.bfloat16), total[:, hidden:].astype(jnp.bfloat16))


def solution(mesh):
    return jax.shard_map(
        on_device,
        mesh=mesh,
        in_specs=(P("dp", "fsdp", None, None), P(), P("dp", "fsdp"), P("fsdp", "dp")),
        out_specs=(P("fsdp", "dp"), P("fsdp", "dp")),
        check_vma=False,
    )
```

time: 796 us -> 428 us (0.54); the launches traced: 785 us -> 428 us
  local copies, waits for them, and re-layouts: 236 us -> 14.5 us
  waiting for transfers between devices: 409 us -> 325 us
  other arithmetic: 71.5 us -> 3.77 us
  Pallas kernels: 0 us -> 27.3 us
  between operations: 26.7 us -> 15.2 us
    psum x1 -> x0, waiting for transfers between devices: 200 us -> none  [on_device(): lax.psum(partial_term.astype(jnp.bfloat16), 'fsdp').astype(jnp.float32)]
    dynamic_update_slice x7 -> x0, local copies, waits for them, and re-layouts: 114 us -> none  [the longest x6 68.8 us: on_device(): lax.dynamic_update_slice(layer_slab, current + incoming[source], (row_off...]
    reduce_scatter x0 -> x1, waiting for transfers between devices: none -> 102 us  [on_device(): lax.psum_scatter(partial_term.astype(jnp.bfloat16), 'fsdp', scatter_dimen...]
    all_gather x2, waiting for transfers between devices: 58.1 us -> 99.9 us  [the longest x1 99.9 us: on_device(): grads_in = lax.all_gather(grads_own, 'fsdp', axis=0, tiled=True)]
    ppermute x1, waiting for transfers between devices: 47.7 us -> 7.03 us  [from_ahead(): lax.ppermute(value, axis, [(source, source - steps) for source in range(s...]
    pallas_call x0 -> x2, Pallas kernels: none -> 27.3 us  [the longest x1 17.1 us: pack(): pl.pallas_call(functools.partial(pack_kernel, row_units=row_units), out_s...]
    slice x12 -> x3, local copies, waits for them, and re-layouts: 23.7 us -> 1.24 us  [the longest x1 0.7 us: on_device(): firsts = shard_table[:, 0].reshape(2, n_feature, per_block)]
    select_n x1 -> x0, other arithmetic: 21.9 us -> none  [on_device(): jnp.where(live[:, None], old_shards[0, 0], jnp.zeros((), jnp.bfloat16))]
  transfers between devices with their start and end apart: 5 -> 5, of which waited for: 4 -> 4; matrix products, arithmetic and copies ran while one was open for 22% -> 0% of each run, Pallas kernels for 0% -> 2%
where the time goes in v1:
time: 428 us
  waiting for transfers between devices  325 us (76%)
  matrix products  33.7 us (8%)
  Pallas kernels  27.3 us (6%)
  between operations  15.2 us (4%)
  local copies, waits for them, and re-layouts  14.5 us (3%)
  starting transfers between devices  8.01 us (2%)
    all_to_all x1, waiting for transfers between devices, on_device(): lax.all_to_all(outgoing, 'dp', split_axis=0, concat_axis=0, tiled=True)  117 us
    reduce_scatter x1, waiting for transfers between devices, on_device(): lax.psum_scatter(partial_term.astype(jnp.bfloat16), 'fsdp', scatter_dimen...  102 us
    all_gather x1, waiting for transfers between devices, on_device(): grads_in = lax.all_gather(grads_own, 'fsdp', axis=0, tiled=True)  99.9 us
    dot_general x1, matrix products, on_device(): partial_term = jnp.dot(all_rows, joined, preferred_element_type=jnp.float32)  21.9 us
    pallas_call x1, Pallas kernels, pack(): pl.pallas_call(functools.partial(pack_kernel, row_units=row_units), out_s...  17.1 us
    dot_general x1, matrix products, on_device(): lax.dot_general(all_rows[:, :block_rows], grads_in, (((0,), (0,)), ((), (...  11.8 us
    pallas_call x1, Pallas kernels, unpack(): pl.pallas_call(functools.partial(unpack_kernel, per_matrix=per_matrix), o...  10.2 us
    unnamed x10, local copies, waits for them, and re-layouts  10.2 us
  transfers between devices with their start and end apart: 5, of which 4 were waited for; matrix products, arithmetic and copies ran while one was open for 0% of the time, Pallas kernels for 2%

profile of v1, /device:TPU:1, one launch (start us, length us, event | category | flops | bytes accessed | tf_op | source)
XLA Modules:
  0.0 427.6 jit_solution(18371954649030361403)
XLA Ops:
  7.2 0.8 constant_dynamic-slice_fusion
  8.0 0.5 fusion.9
  9.8 0.1 pad_add_fusion.place_ref
  9.9 3.8 copy-done.1
  13.7 17.1 %shard_map.59 = bf16[8,352,1792]{2,1,0:T(8,128)(2,1)S(1)} custom-call(s32[2]{0:T(128)S(1)} %pad_add_fusion.place_ref, bf16[38230,128]{1,0:T(8,128)(2,1)S(1)} %bitcast.8), custom_call_target="tpu_custom_call" | custom-call | bytes 19573760 | tf_op jit(solution)/shard_map/pallas_call | solution.py:50
  30.8 3.8 copy-done
  34.6 6.6 %all-to-all-start = ((bf16[8,352,1792]{2,1,0:T(8,128)(2,1)}), bf16[8,352,1792]{2,1,0:T(8,128)(2,1)}, u32[]{:S(2)}, u32[]{:S(2)}) async-start(bf16[8,352,1792]{2,1,0:T(8,128)(2,1)} %copy-done), calls=%async_computation | async-start | bytes 20185088 | tf_op jit(solution)/shard_map/all_to_all | solution.py:131
  41.2 0.0 copy-done.3
  41.2 1.3 collective-permute-start
  42.5 7.0 %collective-permute-done = bf16[256,384]{1,0:T(8,128)(2,1)S(1)} collective-permute-done((bf16[256,384]{1,0:T(8,128)(2,1)S(1)}, bf16[256,384]{1,0:T(8,128)(2,1)S(1)}, u32[]{:S(2)}, u32[]{:S(2)}) %collective-permute-start) | collective-permute-done | bytes 196640 | tf_op jit(solution)/shard_map/ppermute | solution.py:17
  49.6 0.8 pad_maximum_fusion.1
  50.4 0.0 all-gather.3.cloned.1.call-update
  50.4 0.0 reduce-scatter.2.cloned.1.call-start
  50.4 0.7 slice_reduce_fusion
  51.1 0.1 reshape_squeeze.3
  51.3 0.1 div.27
  51.4 0.1 and.25
  51.5 116.6 %all-to-all-done.slab_ref = bf16[8,352,1792]{2,1,0:T(8,128)(2,1)} async-done(((bf16[8,352,1792]{2,1,0:T(8,128)(2,1)}), bf16[8,352,1792]{2,1,0:T(8,128)(2,1)}, u32[]{:S(2)}, u32[]{:S(2)}) %all-to-all-start) | async-done | bytes 10092576 | tf_op jit(solution)/shard_map/all_to_all | solution.py:131
  168.1 10.2 %shard_map.60 = bf16[896,3584]{1,0:T(8,128)(2,1)S(1)} custom-call(s32[6]{0:T(128)S(1)} %fusion.7.offset_ref, bf16[8,352,1792]{2,1,0:T(8,128)(2,1)} %all-to-all-done.slab_ref), custom_call_target="tpu_custom_call" | custom-call | bytes 16515072 | tf_op jit(solution)/shard_map/pallas_call | solution.py:81
  178.3 0.0 copy-start.2
  178.3 2.6 copy-done.2
  180.9 21.9 %convolution_convert_fusion = bf16[2048,3584]{1,0:T(8,128)(2,1)} fusion(bf16[2048,896]{1,0:T(8,128)(2,1)} %all-gather.3.cloned.1.call-done, bf16[896,3584]{1,0:T(8,128)(2,1)} %copy-done.2), kind=kOutput, calls=%fused_computation | convolution fusion | flops 13160677376 | bytes 24772608 | tf_op jit(solution)/shard_map/dot_general | solution.py:142
  202.8 0.0 reduce-scatter.2.cloned.1.call-update
  202.8 0.0 all-gather.5.cloned.1.call-start
  202.9 101.5 %reduce-scatter.2.cloned.1.call-done = bf16[128,3584]{1,0:T(8,128)(2,1)} async-done(((bf16[2048,3584]{1,0:T(8,128)(2,1)}), bf16[128,3584]{1,0:T(8,128)(2,1)}) %reduce-scatter.2.cloned.1.call-update) | async-done | bytes 917520 | tf_op jit(solution)/shard_map/reduce_scatter | solution.py:143
  304.4 1.4 convert_element_type.14
  305.8 0.5 fusion.3
  306.2 1.0 pad_maximum_fusion
  307.2 0.0 all-gather.5.cloned.1.call-update
  307.3 99.9 %all-gather.5.cloned.1.call-done = bf16[2048,3584]{1,0:T(8,128)(2,1)} async-done(((bf16[128,3584]{1,0:T(8,128)(2,1)}), bf16[2048,3584]{1,0:T(8,128)(2,1)}) %all-gather.5.cloned.1.call-update) | async-done | bytes 14680080 | tf_op jit(solution)/shard_map/all_gather | solution.py:147
  407.2 11.8 %convolution_convert_fusion.1 = bf16[512,3584]{1,0:T(8,128)(2,1)S(1)} fusion(bf16[2048,3584]{1,0:T(8,128)(2,1)} %all-gather.5.cloned.1.call-done, bf16[2048,896]{1,0:T(8,128)(2,1)} %all-gather.3.cloned.1.call-done), kind=kOutput, calls=%fused_computation.1 | convolution fusion | flops 7518027776 | bytes 20447232 | tf_op jit(solution)/shard_map/dot_general | solution.py:148
  419.0 2.1 fusion.8
  (11 shorter events, 0.1 us)
Async XLA Ops:
  9.9 3.8 copy-start.1
  30.8 3.8 copy-start
  34.5 6.6 %copy-start.3 = (bf16[256,512]{1,0:T(8,128)(2,1)S(1)}, bf16[256,512]{1,0:T(8,128)(2,1)}, u32[]{:S(2)}) copy-start(bf16[256,512]{1,0:T(8,128)(2,1)} %param.6) | copy-start | bytes 786436
  34.6 133.5 %all-to-all-start = ((bf16[8,352,1792]{2,1,0:T(8,128)(2,1)}), bf16[8,352,1792]{2,1,0:T(8,128)(2,1)}, u32[]{:S(2)}, u32[]{:S(2)}) async-start(bf16[8,352,1792]{2,1,0:T(8,128)(2,1)} %copy-done), calls=%async_computation | async-start | bytes 20185088 | tf_op jit(solution)/shard_map/all_to_all | solution.py:131
  41.2 139.7 %all-gather.3.cloned.1.call-start = ((), (), s32[]{:S(2)}) async-start(), calls=%async_computation.2 | async-start | bytes 4128768 | tf_op jit(solution)/shard_map/all_gather | solution.py:135
  41.2 8.3 %collective-permute-start = (bf16[256,384]{1,0:T(8,128)(2,1)S(1)}, bf16[256,384]{1,0:T(8,128)(2,1)S(1)}, u32[]{:S(2)}, u32[]{:S(2)}) collective-permute-start(bf16[256,384]{1,0:T(8,128)(2,1)S(1)} %slice.31), channel_id=1, source_target_pairs={{1,0},{2,1},{3,2},{4,3},{5,4},{6,5},{7,6},{8,7},{9,8},{10,9},{11,1... | collective-permute-start | bytes 589832 | tf_op jit(solution)/shard_map/ppermute | solution.py:17
  50.4 254.0 %reduce-scatter.2.cloned.1.call-start = ((), (), s32[]{:S(2)}) async-start(), calls=%async_computation.3 | async-start | bytes 15597568 | tf_op jit(solution)/shard_map/reduce_scatter | solution.py:143
  178.3 2.6 copy-start.2
  202.8 103.0 %copy-start.4 = (bf16[128,1792]{1,0:T(8,128)(2,1)S(1)}, bf16[128,1792]{1,0:T(8,128)(2,1)}, u32[]{:S(2)}) copy-start(bf16[128,1792]{1,0:T(8,128)(2,1)} %param.7) | copy-start | bytes 1376260
  202.8 204.3 %all-gather.5.cloned.1.call-start = ((), (), s32[]{:S(2)}) async-start(), calls=%async_computation.4 | async-start | bytes 15597568 | tf_op jit(solution)/shard_map/all_gather | solution.py:147
Sparse Core Ops, SparseCore 0:
  50.5 51.2 all-gather.2
  203.0 101.4 reduce-scatter.1
  307.4 99.7 all-gather.4

commit v2 on v1

v2 whole, which is shorter than its diff:
```python
import functools

import jax
import jax.numpy as jnp
from jax import lax
from jax.experimental import pallas as pl
from jax.experimental.pallas import tpu as pltpu
from jax.sharding import PartitionSpec as P

LANES = 128
GROUP = 32
ALIGN = 8
SIDE = 4
PER_MATRIX = 3
CHUNKS = ((4, 2), (4, 4))
ORDER = "u0 f0 u1 s0 f1 b0 s1 b1".split()
BRIEF = pl.CostEstimate(flops=1, bytes_accessed=1, transcendentals=0)
VMEM = pltpu.CompilerParams(vmem_limit_bytes=60 * 1024 * 1024)


def full(shape):
    return pl.BlockSpec(shape, lambda *_: (0,) * len(shape))


def low_half(shape):
    return lax.broadcasted_iota(jnp.int32, shape, len(shape) - 1) < LANES // 2


def segments(chunk):
    found, unit, lane = [], 0, 0
    for count in chunk:
        found.append((count, unit, lane))
        unit += count
        lane += 2 * LANES * count // SIDE
    return found


def piece_width(chunk):
    return 2 * LANES * sum(chunk) // SIDE


def swap_halves(value):
    return pltpu.roll(value, LANES // 2, value.ndim - 1)


def pack_kernel(place_ref, shard_ref, *refs, row_units, base):
    out_refs, units = refs[:-1], refs[-1]
    group = pl.program_id(0)
    lead = place_ref[0]
    length = place_ref[1]
    block = GROUP * row_units
    held = ALIGN * row_units
    n_owner = out_refs[0].shape[0]
    owned = row_units // n_owner

    @pl.when(group == 0)
    def _():
        units[:held] = jnp.zeros((held, LANES), jnp.float32)

    @pl.when(group > 0)
    def _():
        units[:held] = units[block : block + held]

    whole = (group + 1) * block <= length

    @pl.when(whole)
    def _():
        units[held:] = shard_ref[...].astype(jnp.float32)

    @pl.when(jnp.logical_not(whole))
    def _():
        position = group * block + lax.broadcasted_iota(jnp.int32, (block, LANES), 0)
        units[held:] = jnp.where(position < length, shard_ref[...].astype(jnp.float32), 0.0)

    for owner in range(n_owner):
        column = owner * owned + base
        for out_ref in out_refs:
            for unit in range(out_ref.shape[2] // LANES):
                rows = units[pl.ds(held - lead + column, GROUP, stride=row_units), :]
                out_ref[owner, :, unit * LANES : (unit + 1) * LANES] = rows.astype(out_ref.dtype)
                column += 1


def pack(place, shard, n_owner, row_units, slab_rows, base, chunks):
    block = GROUP * row_units
    last = pl.cdiv(shard.shape[0], block) - 1
    return pl.pallas_call(
        functools.partial(pack_kernel, row_units=row_units, base=base),
        out_shape=[
            jax.ShapeDtypeStruct((n_owner, slab_rows, sum(n) * LANES), shard.dtype) for n in chunks
        ],
        grid_spec=pltpu.PrefetchScalarGridSpec(
            num_scalar_prefetch=1,
            grid=(slab_rows // GROUP,),
            in_specs=[pl.BlockSpec((block, LANES), lambda g, _: (jnp.minimum(g, last), 0))],
            out_specs=[
                pl.BlockSpec((n_owner, GROUP, sum(n) * LANES), lambda g, _: (0, g, 0)) for n in chunks
            ],
            scratch_shapes=[pltpu.VMEM((block + ALIGN * row_units, LANES), jnp.float32)],
        ),
        compiler_params=VMEM,
        cost_estimate=BRIEF,
    )(place, shard)


def unpack_kernel(meta_ref, slab_ref, *refs, chunk):
    out_refs, total = refs[:SIDE], refs[SIDE]
    slab_rows = slab_ref.shape[1]
    side = meta_ref[2 * PER_MATRIX]

    def gathered(matrix, tile):
        total[...] = jnp.zeros_like(total)
        for source in range(matrix * PER_MATRIX, (matrix + 1) * PER_MATRIX):
            rows = pl.ds(pl.multiple_of(meta_ref[source], ALIGN), slab_rows)
            lanes = pl.ds(pl.multiple_of(tile * LANES, LANES), LANES)
            total[rows, :] += slab_ref[source, :, lanes].astype(jnp.float32)
        return total[...]

    for step, out_ref in enumerate(out_refs):
        part = lax.rem(side + step, SIDE)
        for count, unit, lane in segments(chunk):
            if count == SIDE:
                for matrix in range(2):
                    lanes = slice(lane + matrix * LANES, lane + (matrix + 1) * LANES)
                    out_ref[:, lanes] = gathered(matrix, unit + part).astype(out_ref.dtype)
            else:
                first = lax.rem(part, 2) == 0
                gate = gathered(0, unit + part // 2)
                gate = jnp.where(first, gate, swap_halves(gate))
                upper = gathered(1, unit + part // 2)
                upper = jnp.where(first, swap_halves(upper), upper)
                value = jnp.where(low_half(gate.shape), gate, upper)
                out_ref[:, lane : lane + LANES] = value.astype(out_ref.dtype)


def unpack(meta, slabs, rows_out, chunk):
    _, slab_rows, width = slabs.shape
    out_width = piece_width(chunk)
    sources = 2 * PER_MATRIX
    return pl.pallas_call(
        functools.partial(unpack_kernel, chunk=chunk),
        out_shape=[jax.ShapeDtypeStruct((rows_out, out_width), slabs.dtype)] * SIDE,
        grid_spec=pltpu.PrefetchScalarGridSpec(
            num_scalar_prefetch=1,
            grid=(1,),
            in_specs=[full((sources, slab_rows, width))],
            out_specs=[full((rows_out, out_width))] * SIDE,
            scratch_shapes=[pltpu.VMEM((rows_out, LANES), jnp.float32)],
        ),
        compiler_params=VMEM,
        cost_estimate=BRIEF,
    )(meta, slabs)


def forward_kernel(meta_ref, *refs):
    own, sibling = refs[:SIDE], refs[SIDE : 2 * SIDE]
    edges = refs[2 * SIDE : 2 * SIDE + 2]
    weights = refs[2 * SIDE + 2 : 3 * SIDE + 2]
    out_refs = refs[3 * SIDE + 2 : 4 * SIDE + 2]
    joined = refs[4 * SIDE + 2]
    piece = pl.program_id(0)
    last = meta_ref[SIDE]
    features = own[0].shape[2]
    spill = edges[0].shape[2]
    rows = own[0].shape[1]

    @pl.when(piece == 0)
    def _():
        beyond = None
        for step, weight in enumerate(weights):
            source = (step + 1) % SIDE
            tail = weights[source][features:].astype(jnp.float32)
            inside = jnp.where(last == source, 0.0, tail)
            outside = tail - inside
            beyond = outside if beyond is None else beyond + outside
            head = weight[:spill].astype(jnp.float32) + inside
            first = step * features
            joined[first : first + spill] = head.astype(joined.dtype)
            joined[first + spill : first + features] = weight[spill:features]
        joined[SIDE * features :] = beyond.astype(joined.dtype)

    for half, (parts, edge) in enumerate(((own, edges[0]), (sibling, edges[1]))):
        left = jnp.concatenate([part[0] for part in parts] + [edge[0]], axis=1)
        value = jnp.dot(left, joined[...], preferred_element_type=jnp.float32)
        value = value.astype(jnp.bfloat16)
        for index, out_ref in enumerate(out_refs):

            @pl.when(piece == index)
            def _():
                out_ref[half * rows : (half + 1) * rows] = value


def forward(meta, tokens, edges, weights):
    _, rows, features = tokens[0].shape
    spill = edges.shape[2]
    width = weights[0].shape[1]
    depth = SIDE * features + spill
    block = pl.BlockSpec((1, rows, features), lambda p, m: (m[p], 0, 0))
    edge = lambda first: pl.BlockSpec((1, rows, spill), lambda p, m: (m[first + p], 0, 0))
    return pl.pallas_call(
        forward_kernel,
        out_shape=[jax.ShapeDtypeStruct((2 * rows, width), jnp.bfloat16)] * SIDE,
        grid_spec=pltpu.PrefetchScalarGridSpec(
            num_scalar_prefetch=1,
            grid=(SIDE,),
            in_specs=[block] * (2 * SIDE)
            + [edge(SIDE + 1), edge(2 * SIDE + 1)]
            + [full(weights[0].shape)] * SIDE,
            out_specs=[full((2 * rows, width))] * SIDE,
            scratch_shapes=[pltpu.VMEM((depth, width), jnp.bfloat16)],
        ),
        compiler_params=VMEM,
        cost_estimate=BRIEF,
    )(meta, *tokens, edges, edges, *weights)


def swiglu_kernel(meta_ref, *refs, base, chunk):
    parts, upstream_ref, out_ref = refs[:SIDE], refs[SIDE], refs[SIDE + 1]
    side = meta_ref[1]
    first = lax.rem(side, 2) == 0
    for count, unit, lane in segments(chunk):
        tile = base + unit + (side if count == SIDE else side // 2)
        width = 2 * LANES * count // SIDE
        summed = parts[0][:, lane : lane + width].astype(jnp.float32)
        for part in parts[1:]:
            summed += part[:, lane : lane + width].astype(jnp.float32)
        lanes = pl.ds(pl.multiple_of(tile * LANES, LANES), LANES)
        incoming = upstream_ref[:, lanes].astype(jnp.float32)
        if count == SIDE:
            gate, upper = summed[:, :LANES], summed[:, LANES:]
        else:
            low = low_half(summed.shape)
            swapped = swap_halves(summed)
            gate = jnp.where(low, summed, swapped)
            upper = jnp.where(low, swapped, summed)
            incoming = jnp.where(low == first, incoming, swap_halves(incoming))
        sigma = jax.nn.sigmoid(gate)
        grad_gate = incoming * upper * sigma * (1.0 + gate * (1.0 - sigma))
        grad_upper = incoming * gate * sigma
        if count == SIDE:
            out_ref[:, lane : lane + LANES] = grad_gate.astype(out_ref.dtype)
            out_ref[:, lane + LANES : lane + width] = grad_upper.astype(out_ref.dtype)
        else:
            value = jnp.where(low, grad_gate, grad_upper)
            out_ref[:, lane : lane + LANES] = value.astype(out_ref.dtype)


def swiglu_backward(meta, parts, upstream, base, chunk):
    rows, width = parts[0].shape
    half = pl.BlockSpec((rows // 2, width), lambda h, m: (h, 0))
    return pl.pallas_call(
        functools.partial(swiglu_kernel, base=base, chunk=chunk),
        out_shape=jax.ShapeDtypeStruct((rows, width), jnp.bfloat16),
        grid_spec=pltpu.PrefetchScalarGridSpec(
            num_scalar_prefetch=1,
            grid=(2,),
            in_specs=[half] * SIDE
            + [
                pl.BlockSpec(
                    (rows // 2, upstream.shape[1]), lambda h, m: (lax.rem(h + m[0], 2), 0)
                )
            ],
            out_specs=half,
        ),
        compiler_params=VMEM,
        cost_estimate=BRIEF,
    )(meta, *parts, upstream)


def backward_kernel(meta_ref, *refs):
    sources = refs[: 2 * SIDE]
    grads = refs[2 * SIDE : 3 * SIDE]
    out_refs = refs[3 * SIDE : 4 * SIDE]
    held, turned, arrived = refs[4 * SIDE :]
    rows = held.shape[2]
    copies = [
        pltpu.make_async_copy(source, held.at[index], arrived.at[index])
        for index, source in enumerate(sources)
    ]
    for step in range(SIDE):
        copies[step].start()
        copies[step + SIDE].start()
    for step, grad in enumerate(grads):
        turned[meta_ref[step]] = grad[...].astype(jnp.float32).T.astype(turned.dtype)
    left = jnp.concatenate(
        [turned[t, :, :rows] for t in range(SIDE)] + [turned[t, :, rows:] for t in range(SIDE)],
        axis=1,
    )
    for step, out_ref in enumerate(out_refs):
        copies[step].wait()
        copies[step + SIDE].wait()
        right = jnp.concatenate(
            [held[step, t] for t in range(SIDE)] + [held[step + SIDE, t] for t in range(SIDE)],
            axis=0,
        )
        total = jnp.dot(left, right, preferred_element_type=jnp.float32)
        out_ref[...] = total.T.astype(out_ref.dtype)


def backward(meta, tokens, grads):
    blocks, rows, features = tokens[0].shape
    width = grads[0].shape[1]
    return pl.pallas_call(
        backward_kernel,
        out_shape=[jax.ShapeDtypeStruct((features, width), jnp.bfloat16)] * SIDE,
        grid_spec=pltpu.PrefetchScalarGridSpec(
            num_scalar_prefetch=1,
            grid=(1,),
            in_specs=[pl.BlockSpec(memory_space=pl.ANY)] * (2 * SIDE)
            + [full((2 * rows, width))] * SIDE,
            out_specs=[full((features, width))] * SIDE,
            scratch_shapes=[
                pltpu.VMEM((2 * SIDE, blocks, rows, features), jnp.bfloat16),
                pltpu.VMEM((SIDE, width, 2 * rows), jnp.bfloat16),
                pltpu.SemaphoreType.DMA((2 * SIDE,)),
            ],
        ),
        compiler_params=VMEM,
        cost_estimate=BRIEF,
    )(meta, *tokens, *grads)


def assemble_kernel(meta_ref, *refs):
    parts = refs[: SIDE * len(CHUNKS)]
    gate_ref, upper_ref, held = refs[SIDE * len(CHUNKS) :]
    side = meta_ref[0]
    base = 0
    for index, chunk in enumerate(CHUNKS):
        pieces = parts[SIDE * index : SIDE * (index + 1)]
        for count, unit, lane in segments(chunk):
            if count == SIDE:
                for step, piece in enumerate(pieces):
                    tile = base + unit + lax.rem(side + step, SIDE)
                    lanes = pl.ds(pl.multiple_of(tile * LANES, LANES), LANES)
                    gate_ref[:, lanes] = piece[:, lane : lane + LANES]
                    upper_ref[:, lanes] = piece[:, lane + LANES : lane + 2 * LANES]
            else:
                for step, piece in enumerate(pieces):
                    value = piece[:, lane : lane + LANES].astype(jnp.float32)
                    held[lax.rem(side + step, SIDE)] = value
                for pair in range(2):
                    left, right = held[2 * pair], held[2 * pair + 1]
                    low = low_half(left.shape)
                    first = (base + unit + pair) * LANES
                    gate = jnp.where(low, left, swap_halves(right))
                    upper = jnp.where(low, swap_halves(left), right)
                    gate_ref[:, first : first + LANES] = gate.astype(gate_ref.dtype)
                    upper_ref[:, first : first + LANES] = upper.astype(upper_ref.dtype)
        base += sum(chunk)


def assemble(meta, pieces, hidden):
    rows = pieces[0].shape[0]
    block = rows // 4
    out = pl.BlockSpec((block, hidden), lambda r, m: (r, 0))
    return pl.pallas_call(
        assemble_kernel,
        out_shape=[jax.ShapeDtypeStruct((rows, hidden), jnp.bfloat16)] * 2,
        grid_spec=pltpu.PrefetchScalarGridSpec(
            num_scalar_prefetch=1,
            grid=(rows // block,),
            in_specs=[
                pl.BlockSpec((block, piece.shape[1]), lambda r, m: (r, 0)) for piece in pieces
            ],
            out_specs=[out, out],
            scratch_shapes=[pltpu.VMEM((SIDE, block, LANES), jnp.float32)],
        ),
        compiler_params=VMEM,
        cost_estimate=BRIEF,
    )(meta, *pieces)


def along_z(value, steps):
    pairs = [
        (z * SIDE + x, (z + steps) % SIDE * SIDE + x) for z in range(SIDE) for x in range(SIDE)
    ]
    return lax.ppermute(value, "fsdp", pairs)


def along_x(value, steps):
    pairs = [
        (z * SIDE + x, z * SIDE + (x + steps) % SIDE) for z in range(SIDE) for x in range(SIDE)
    ]
    return lax.ppermute(value, "fsdp", pairs)


def along_y(value, steps):
    pairs = [(2 * y + c, (y + steps) % SIDE * 2 + c) for y in range(SIDE) for c in range(2)]
    return lax.ppermute(value, "dp", pairs)


def to_sibling(value):
    return lax.ppermute(value, "dp", [(d, d ^ 1) for d in range(2 * SIDE)])


def stacked_over_y(value):
    return jnp.stack([value] + [along_y(value, t) for t in range(1, SIDE)])


def after(value, *earlier):
    return lax.optimization_barrier((value, earlier))[0]


def exchange(slabs):
    return lax.all_to_all(slabs, "dp", split_axis=0, concat_axis=0, tiled=True)


def features_ahead(tokens, spill):
    pairs = [((z + 1) * SIDE, z * SIDE) for z in range(SIDE - 1)]
    return lax.ppermute(tokens[:, :spill], "fsdp", pairs)


def from_first_x(ahead):
    edge = ahead
    for x in range(1, SIDE):
        edge += lax.ppermute(ahead, "fsdp", [(z * SIDE, z * SIDE + x) for z in range(SIDE)])
    return edge


def on_device(old_shards, shard_table, tokens, cotangent):
    n_data = lax.axis_size("dp")
    n_feature = lax.axis_size("fsdp")
    data_index = lax.axis_index("dp")
    feature_index = lax.axis_index("fsdp")
    y, core = data_index // 2, data_index % 2
    z, x = feature_index // SIDE, feature_index % SIDE
    block_rows = tokens.shape[1]
    hidden = cotangent.shape[1]
    row_units = hidden // LANES * n_data
    capacity = old_shards.shape[2]
    first_row = feature_index * block_rows
    slab_rows = pl.cdiv(ALIGN * row_units + capacity, GROUP * row_units) * GROUP
    spill = pl.cdiv(slab_rows, LANES) * LANES
    steps = jnp.arange(SIDE, dtype=jnp.int32)

    matrix_id = data_index // PER_MATRIX
    holder = data_index < 2 * PER_MATRIX
    table_row = (matrix_id * n_feature + feature_index) * PER_MATRIX + data_index % PER_MATRIX
    my_entry = lax.dynamic_index_in_dim(
        shard_table, jnp.minimum(table_row, shard_table.shape[0] - 1), 0, keepdims=False
    )
    lead = (my_entry[0] - first_row * row_units) % (ALIGN * row_units)
    place = jnp.stack([lead, jnp.where(holder, my_entry[1], 0)])
    firsts = shard_table[:, 0].reshape(2, n_feature, PER_MATRIX)
    firsts = lax.dynamic_index_in_dim(firsts, feature_index, 1, keepdims=False).reshape(-1)
    offsets = (firsts // row_units - first_row) // ALIGN * ALIGN
    unpack_meta = jnp.concatenate([offsets, x[None]]).astype(jnp.int32)
    edge_block = 2 * ((z + steps) % SIDE)
    forward_meta = jnp.concatenate(
        [(y - z - steps) % SIDE, (x + 1)[None] % SIDE, edge_block + core, edge_block + 1 - core]
    )
    backward_meta = (y - z + steps) % SIDE

    shard = old_shards[0, 0]
    pack_chunks = functools.partial(
        pack, shard=shard, n_owner=n_data, row_units=row_units, slab_rows=slab_rows
    )
    groups = [[z * SIDE + x for x in range(SIDE)] for z in range(SIDE)]
    outgoing = list(pack_chunks(place, base=0, chunks=CHUNKS[:1]))
    rows = stacked_over_y(tokens)
    ahead = features_ahead(tokens, spill)
    outgoing, rows, ahead, place = lax.optimization_barrier((outgoing, rows, ahead, place))
    incoming = [exchange(outgoing[0])]
    outgoing += list(pack_chunks(place, base=sum(CHUNKS[0]), chunks=CHUNKS[1:]))
    gathered = [rows] + [along_x(rows, s) for s in range(1, SIDE)]
    edge = from_first_x(after(ahead, outgoing[1]))
    edges = lax.all_gather(edge, "dp", axis=0)
    sibling = [to_sibling(part) for part in gathered]
    outgoing, gathered, edge = lax.optimization_barrier((outgoing, gathered, edge))
    gathered = gathered + sibling
    for slabs in outgoing[1:]:
        incoming.append(exchange(after(slabs, incoming[-1])))

    weights, parts, grads, pieces = {}, {}, {}, {}
    latest = outgoing[1]
    for step in ORDER:
        index = int(step[1])
        chunk = CHUNKS[index]
        base = sum(sum(earlier) for earlier in CHUNKS[:index])
        if step[0] == "u":
            slabs = after(incoming[index], latest, sibling)
            columns = unpack(unpack_meta, slabs, block_rows + spill, chunk)
            weights[index] = [columns[0]] + [along_x(columns[s], s) for s in range(1, SIDE)]
            if index == 0:
                upstream = lax.all_gather(
                    after(cotangent, weights[0]), "fsdp", axis=0, tiled=True, axis_index_groups=groups
                )
            latest = columns[0]
        if step[0] == "f":
            own = [after(weights[index][0], latest)] + weights[index][1:]
            partial = forward(forward_meta, gathered, edges, own)
            parts[index] = [partial[0]] + [along_z(partial[s], s) for s in range(1, SIDE)]
            latest = partial[0]
        if step[0] == "s":
            own = [after(parts[index][0], latest)] + parts[index][1:]
            swiglu_meta = jnp.stack([core, x]).astype(jnp.int32)
            latest = swiglu_backward(swiglu_meta, own, upstream, base, chunk)
            grads[index] = [latest] + [along_z(latest, s) for s in range(1, SIDE)]
        if step[0] == "b":
            own = [after(grads[index][0], latest, pieces)] + grads[index][1:]
            sums = backward(backward_meta, gathered, own)
            pieces[index] = [sums[0]] + [along_x(sums[s], -s) for s in range(1, SIDE)]
            latest = sums[0]
    finished = [piece for index in range(len(CHUNKS)) for piece in pieces[index]]
    return tuple(assemble(x[None], finished, hidden))


def solution(mesh):
    return jax.shard_map(
        on_device,
        mesh=mesh,
        in_specs=(P("dp", "fsdp", None, None), P(), P("dp", "fsdp"), P("fsdp", "dp")),
        out_specs=(P("fsdp", "dp"), P("fsdp", "dp")),
        check_vma=False,
    )
```

time: 428 us -> 354 us (0.83)
  waiting for transfers between devices: 325 us -> 157 us
  Pallas kernels: 27.3 us -> 97.7 us
  starting transfers between devices: 8.01 us -> 70.3 us
  matrix products: 33.7 us -> 0 us
  local copies, waits for them, and re-layouts: 14.5 us -> 8.68 us
    ppermute x1 -> x38, waiting for transfers between devices: 7.03 us -> 147 us  [the longest x15 80.9 us: along_x(): return lax.ppermute(value, 'fsdp', pairs)]
    all_to_all x1 -> x2, waiting for transfers between devices: 117 us -> 8.55 us  [exchange(): return lax.all_to_all(slabs, 'dp', split_axis=0, concat_axis=0, tiled=True)]
    reduce_scatter x1 -> x0, waiting for transfers between devices: 102 us -> none  [on_device(): lax.psum_scatter(partial_term.astype(jnp.bfloat16), 'fsdp', scatter_dimen...]
    all_gather x2, waiting for transfers between devices: 99.9 us -> 0.01 us  [the longest x1 0.01 us: on_device(): edges = lax.all_gather(edge, 'dp', axis=0)]
    pallas_call x2 -> x11, Pallas kernels: 27.3 us -> 97.7 us  [the longest x2 28.2 us: pack(): pl.pallas_call(functools.partial(pack_kernel, row_units=row_units, base=b...]
    ppermute x1 -> x38, starting transfers between devices: 1.29 us -> 58.5 us  [the longest x15 22.3 us: along_x(): return lax.ppermute(value, 'fsdp', pairs)]
    dot_general x2 -> x0, matrix products: 33.7 us -> none  [the longest x1 21.9 us: on_device(): partial_term = jnp.dot(all_rows, joined, preferred_element_type=jnp.float32)]
    all_to_all x1 -> x2, starting transfers between devices: 6.63 us -> 11.8 us  [exchange(): return lax.all_to_all(slabs, 'dp', split_axis=0, concat_axis=0, tiled=True)]
  transfers between devices with their start and end apart: 5 -> 42, of which waited for: 4 -> 19; matrix products, arithmetic and copies ran while one was open for 0% -> 2% of each run, Pallas kernels for 2% -> 23%
where the time goes in v2:
time: 354 us; the launch traced here: 353 us
  waiting for transfers between devices  157 us (44%)
  Pallas kernels  97.7 us (28%)
  starting transfers between devices  70.3 us (20%)
  between operations  15.7 us (4%)
  local copies, waits for them, and re-layouts  8.68 us (2%)
  other arithmetic  3.99 us (1%)
    ppermute x15, waiting for transfers between devices, along_x(): return lax.ppermute(value, 'fsdp', pairs)  80.9 us
    ppermute x3, waiting for transfers between devices, from_first_x(): lax.ppermute(ahead, 'fsdp', [(z * SIDE, z * SIDE + x) for z in range(SIDE)])  31.7 us
    ppermute x12, waiting for transfers between devices, along_z(): return lax.ppermute(value, 'fsdp', pairs)  30.2 us
    pallas_call x2, Pallas kernels, pack(): pl.pallas_call(functools.partial(pack_kernel, row_units=row_units, base=b...  28.2 us
    pallas_call x2, Pallas kernels, forward(): pl.pallas_call(forward_kernel, out_shape=[jax.ShapeDtypeStruct((2 * rows,...  25.7 us
    ppermute x15, starting transfers between devices, along_x(): return lax.ppermute(value, 'fsdp', pairs)  22.3 us
    ppermute x12, starting transfers between devices, along_z(): return lax.ppermute(value, 'fsdp', pairs)  21.2 us
    pallas_call x2, Pallas kernels, backward(): pl.pallas_call(backward_kernel, out_shape=[jax.ShapeDtypeStruct((features...  18.5 us
  transfers between devices with their start and end apart: 42, of which 19 were waited for; matrix products, arithmetic and copies ran while one was open for 2% of the time, Pallas kernels for 23%

profile of v2, /device:TPU:1, one launch (start us, length us, event | category | flops | bytes accessed | tf_op | source)
XLA Modules:
  0.0 353.0 jit_solution(2008842023968839318)
XLA Ops:
  7.2 3.8 %collective-permute-start.1 = (bf16[256,512]{1,0:T(8,128)(2,1)}, bf16[256,512]{1,0:T(8,128)(2,1)S(1)}, u32[]{:S(2)}, u32[]{:S(2)}) collective-permute-start(bf16[256,512]{1,0:T(8,128)(2,1)} %param.6), channel_id=1, source_target_pairs={{0,64},{16,80},{32,96},{48,112},{64,0},{80,16},{96,32},{112,48},{1... | collective-permute-start | bytes 786440 | tf_op jit(solution)/shard_map/ppermute | solution.py:389
  19.2 13.6 %shard_map.59 = bf16[8,352,768]{2,1,0:T(8,128)(2,1)} custom-call(s32[2]{0:T(128)} %pad_add_fusion.place_ref, bf16[38230,128]{1,0:T(8,128)(2,1)} %bitcast.13), custom_call_target="tpu_custom_call" | custom-call | flops 1 | bytes 1 | tf_op jit(solution)/shard_map/pallas_call | solution.py:87
  33.0 5.6 %all-to-all-start = ((bf16[8,352,768]{2,1,0:T(8,128)(2,1)}), bf16[8,352,768]{2,1,0:T(8,128)(2,1)}, u32[]{:S(2)}, u32[]{:S(2)}) async-start(bf16[8,352,768]{2,1,0:T(8,128)(2,1)} %shard_map.59), calls=%async_computation | async-start | bytes 8650752 | tf_op jit(solution)/shard_map/all_to_all | solution.py:405
  42.0 14.6 %shard_map.60 = bf16[8,352,1024]{2,1,0:T(8,128)(2,1)} custom-call(s32[2]{0:T(128)} %pad_add_fusion.place_ref, bf16[38230,128]{1,0:T(8,128)(2,1)} %bitcast.14), custom_call_target="tpu_custom_call" | custom-call | flops 1 | bytes 1 | tf_op jit(solution)/shard_map/pallas_call | solution.py:87
  56.5 3.5 collective-permute-start.9
  61.3 28.2 %collective-permute-done.9 = bf16[256,384]{1,0:T(8,128)(2,1)S(1)} collective-permute-done((bf16[256,384]{1,0:T(8,128)(2,1)S(1)}, bf16[256,384]{1,0:T(8,128)(2,1)S(1)}, u32[]{:S(2)}, u32[]{:S(2)}) %collective-permute-start.9) | collective-permute-done | bytes 196640 | tf_op jit(solution)/shard_map/ppermute | solution.py:416
  90.8 3.5 collective-permute-done.7
  95.1 6.2 %all-to-all-start.1 = ((bf16[8,352,1024]{2,1,0:T(8,128)(2,1)}), bf16[8,352,1024]{2,1,0:T(8,128)(2,1)}, u32[]{:S(2)}, u32[]{:S(2)}) async-start(bf16[8,352,1024]{2,1,0:T(8,128)(2,1)} %shard_map.60), calls=%async_computation.1 | async-start | bytes 11534336 | tf_op jit(solution)/shard_map/all_to_all | solution.py:405
  109.5 6.5 %shard_map.61 = (bf16[896,384]{1,0:T(8,128)(2,1)}, bf16[896,384]{1,0:T(8,128)(2,1)}, bf16[896,384]{1,0:T(8,128)(2,1)}, bf16[896,384]{1,0:T(8,128)(2,1)}) custom-call(s32[7]{0:T(128)} %pad_add_fusion.3.meta_ref, bf16[8,352,768]{2,1,0:T(8,128)(2,1)} %all-to-all-done.slab_ref), custom_call_target="tpu_custom_call" | custom-call | flops 1 | bytes 1 | tf_op jit(solution)/shard_map/pallas_call | solution.py:140
  120.6 28.5 %collective-permute-done.14.refs_11_ = bf16[896,384]{1,0:T(8,128)(2,1)S(1)} collective-permute-done((bf16[896,384]{1,0:T(8,128)(2,1)}, bf16[896,384]{1,0:T(8,128)(2,1)S(1)}, u32[]{:S(2)}, u32[]{:S(2)}) %collective-permute-start.14) | collective-permute-done | bytes 688160 | tf_op jit(solution)/shard_map/ppermute | solution.py:384
  150.4 12.6 %shard_map.62 = (bf16[512,384]{1,0:T(8,128)(2,1)}, bf16[512,384]{1,0:T(8,128)(2,1)}, bf16[512,384]{1,0:T(8,128)(2,1)}, bf16[512,384]{1,0:T(8,128)(2,1)}) custom-call(s32[13]{0:T(128)} %pad_add_fusion.2.meta_ref, bf16[4,256,512]{2,1,0:T(8,128)(2,1)} %copy-done, bf16[4,256,512]{2,1,0:T(8,128)(2,1)} %collective-permute-done.4.refs_1_, ...), custom_call_target="tpu_custom_call" | custom-call | flops 1 | bytes 1 | tf_op jit(solution)/shard_map/pallas_call | solution.py:200
  164.9 8.5 %all-to-all-done.1.slab_ref = bf16[8,352,1024]{2,1,0:T(8,128)(2,1)} async-done(((bf16[8,352,1024]{2,1,0:T(8,128)(2,1)}), bf16[8,352,1024]{2,1,0:T(8,128)(2,1)}, u32[]{:S(2)}, u32[]{:S(2)}) %all-to-all-start.1) | async-done | bytes 5767200 | tf_op jit(solution)/shard_map/all_to_all | solution.py:405
  173.4 6.5 %shard_map.63 = (bf16[896,512]{1,0:T(8,128)(2,1)}, bf16[896,512]{1,0:T(8,128)(2,1)}, bf16[896,512]{1,0:T(8,128)(2,1)}, bf16[896,512]{1,0:T(8,128)(2,1)}) custom-call(s32[7]{0:T(128)} %pad_add_fusion.3.meta_ref, bf16[8,352,1024]{2,1,0:T(8,128)(2,1)} %all-to-all-done.1.slab_ref), custom_call_target="tpu_custom_call" | custom-call | flops 1 | bytes 1 | tf_op jit(solution)/shard_map/pallas_call | solution.py:140
  184.5 3.8 %collective-permute-start.18 = (bf16[512,384]{1,0:T(8,128)(2,1)}, bf16[512,384]{1,0:T(8,128)(2,1)S(1)}, u32[]{:S(2)}, u32[]{:S(2)}) collective-permute-start(bf16[512,384]{1,0:T(8,128)(2,1)} %get-tuple-element.68), channel_id=1, source_target_pairs={{0,8},{1,9},{2,10},{3,11},{4,12},{5,13},{6,14},{7,15},{8,0},{9,1},... | collective-permute-start | bytes 1179656 | tf_op jit(solution)/shard_map/ppermute | solution.py:377
  189.4 7.0 %collective-permute-done.18.refs_2_ = bf16[512,384]{1,0:T(8,128)(2,1)S(1)} collective-permute-done((bf16[512,384]{1,0:T(8,128)(2,1)}, bf16[512,384]{1,0:T(8,128)(2,1)S(1)}, u32[]{:S(2)}, u32[]{:S(2)}) %collective-permute-start.18) | collective-permute-done | bytes 393248 | tf_op jit(solution)/shard_map/ppermute | solution.py:377
  196.5 9.4 %collective-permute-done.19.refs_3_ = bf16[512,384]{1,0:T(8,128)(2,1)} collective-permute-done((bf16[512,384]{1,0:T(8,128)(2,1)S(1)}, bf16[512,384]{1,0:T(8,128)(2,1)}, u32[]{:S(2)}, u32[]{:S(2)}) %collective-permute-start.19) | collective-permute-done | bytes 393248 | tf_op jit(solution)/shard_map/ppermute | solution.py:377
  205.9 3.7 %shard_map.64.refs_8_ = bf16[512,384]{1,0:T(8,128)(2,1)} custom-call(s32[2]{0:T(128)} %pad_add_fusion.1.meta_ref, bf16[512,384]{1,0:T(8,128)(2,1)} %get-tuple-element.66.refs_0_, bf16[512,384]{1,0:T(8,128)(2,1)} %copy-done.21, bf16[512,384]{1,0:T(8,128)(2,1)} %copy-done.22, bf16[512,384]{1,0:T(8,128)(2,1)} %collective-permute-done.19.refs_3_, ...), custom_call_target="tpu_custom_call" | custom-call | flops 1 | bytes 1 | tf_op jit(solution)/shard_map/pallas_call | solution.py:251
  209.6 3.3 collective-permute-start.25
  213.2 8.8 %collective-permute-done.20.refs_11_ = bf16[896,512]{1,0:T(8,128)(2,1)S(1)} collective-permute-done((bf16[896,512]{1,0:T(8,128)(2,1)}, bf16[896,512]{1,0:T(8,128)(2,1)S(1)}, u32[]{:S(2)}, u32[]{:S(2)}) %collective-permute-start.20) | collective-permute-done | bytes 917536 | tf_op jit(solution)/shard_map/ppermute | solution.py:384
  225.8 13.1 %shard_map.65 = (bf16[512,512]{1,0:T(8,128)(2,1)}, bf16[512,512]{1,0:T(8,128)(2,1)}, bf16[512,512]{1,0:T(8,128)(2,1)}, bf16[512,512]{1,0:T(8,128)(2,1)}) custom-call(s32[13]{0:T(128)} %pad_add_fusion.2.meta_ref, bf16[4,256,512]{2,1,0:T(8,128)(2,1)} %copy-done, bf16[4,256,512]{2,1,0:T(8,128)(2,1)} %collective-permute-done.4.refs_1_, ...), custom_call_target="tpu_custom_call" | custom-call | flops 1 | bytes 1 | tf_op jit(solution)/shard_map/pallas_call | solution.py:200
  246.0 8.6 %shard_map.66 = (bf16[512,384]{1,0:T(8,128)(2,1)}, bf16[512,384]{1,0:T(8,128)(2,1)}, bf16[512,384]{1,0:T(8,128)(2,1)}, bf16[512,384]{1,0:T(8,128)(2,1)}) custom-call(s32[4]{0:T(128)} %and_select_fusion.3.meta_ref, bf16[4,256,512]{2,1,0:T(8,128)(2,1)} %copy-done, bf16[4,256,512]{2,1,0:T(8,128)(2,1)} %collective-permute-done.4.refs_1_, ...), custom_call_target="tpu_custom_call" | custom-call | flops 1 | bytes 1 | tf_op jit(solution)/shard_map/pallas_call | solution.py:303
  256.2 8.3 %collective-permute-done.30.refs_2_ = bf16[512,512]{1,0:T(8,128)(2,1)S(1)} collective-permute-done((bf16[512,512]{1,0:T(8,128)(2,1)}, bf16[512,512]{1,0:T(8,128)(2,1)S(1)}, u32[]{:S(2)}, u32[]{:S(2)}) %collective-permute-start.30) | collective-permute-done | bytes 524320 | tf_op jit(solution)/shard_map/ppermute | solution.py:377
  266.2 3.7 %shard_map.67.refs_8_ = bf16[512,512]{1,0:T(8,128)(2,1)} custom-call(s32[2]{0:T(128)} %pad_add_fusion.1.meta_ref, bf16[512,512]{1,0:T(8,128)(2,1)} %get-tuple-element.81.refs_0_, bf16[512,512]{1,0:T(8,128)(2,1)} %copy-done.10, bf16[512,512]{1,0:T(8,128)(2,1)} %copy-done.11, bf16[512,512]{1,0:T(8,128)(2,1)} %copy-done.12, ...), custom_call_target="tpu_custom_call" | custom-call | flops 1 | bytes 1 | tf_op jit(solution)/shard_map/pallas_call | solution.py:251
  269.9 3.3 collective-permute-start.34
  277.6 5.9 %collective-permute-done.27.refs_2_ = bf16[512,384]{1,0:T(8,128)(2,1)S(1)} collective-permute-done((bf16[512,384]{1,0:T(8,128)(2,1)S(1)}, bf16[512,384]{1,0:T(8,128)(2,1)S(1)}, u32[]{:S(2)}, u32[]{:S(2)}) %collective-permute-start.27) | collective-permute-done | bytes 393248 | tf_op jit(solution)/shard_map/ppermute | solution.py:384
  283.6 11.2 %collective-permute-done.28.refs_3_ = bf16[512,384]{1,0:T(8,128)(2,1)S(1)} collective-permute-done((bf16[512,384]{1,0:T(8,128)(2,1)S(1)}, bf16[512,384]{1,0:T(8,128)(2,1)S(1)}, u32[]{:S(2)}, u32[]{:S(2)}) %collective-permute-start.28) | collective-permute-done | bytes 393248 | tf_op jit(solution)/shard_map/ppermute | solution.py:384
  295.4 3.9 %collective-permute-done.32.refs_9_ = bf16[512,512]{1,0:T(8,128)(2,1)S(1)} collective-permute-done((bf16[512,512]{1,0:T(8,128)(2,1)}, bf16[512,512]{1,0:T(8,128)(2,1)S(1)}, u32[]{:S(2)}, u32[]{:S(2)}) %collective-permute-start.32) | collective-permute-done | bytes 524320 | tf_op jit(solution)/shard_map/ppermute | solution.py:377
  300.1 9.9 %shard_map.68 = (bf16[512,512]{1,0:T(8,128)(2,1)}, bf16[512,512]{1,0:T(8,128)(2,1)}, bf16[512,512]{1,0:T(8,128)(2,1)}, bf16[512,512]{1,0:T(8,128)(2,1)}) custom-call(s32[4]{0:T(128)} %and_select_fusion.3.meta_ref, bf16[4,256,512]{2,1,0:T(8,128)(2,1)} %copy-done, bf16[4,256,512]{2,1,0:T(8,128)(2,1)} %collective-permute-done.4.refs_1_, ...), custom_call_target="tpu_custom_call" | custom-call | flops 1 | bytes 1 | tf_op jit(solution)/shard_map/pallas_call | solution.py:303
  310.0 3.6 %collective-permute-start.35 = (bf16[512,512]{1,0:T(8,128)(2,1)}, bf16[512,512]{1,0:T(8,128)(2,1)S(1)}, u32[]{:S(2)}, u32[]{:S(2)}) collective-permute-start(bf16[512,512]{1,0:T(8,128)(2,1)} %get-tuple-element.87), channel_id=1, source_target_pairs={{0,3},{1,0},{2,1},{3,2},{4,7},{5,4},{6,5},{7,6},{8,11},{9,8},{10,9... | collective-permute-start | bytes 1572872 | tf_op jit(solution)/shard_map/ppermute | solution.py:384
  314.3 21.5 %collective-permute-done.35.refs_5_ = bf16[512,512]{1,0:T(8,128)(2,1)S(1)} collective-permute-done((bf16[512,512]{1,0:T(8,128)(2,1)}, bf16[512,512]{1,0:T(8,128)(2,1)S(1)}, u32[]{:S(2)}, u32[]{:S(2)}) %collective-permute-start.35) | collective-permute-done | bytes 524320 | tf_op jit(solution)/shard_map/ppermute | solution.py:384
  335.9 4.6 %collective-permute-done.37.refs_7_ = bf16[512,512]{1,0:T(8,128)(2,1)S(1)} collective-permute-done((bf16[512,512]{1,0:T(8,128)(2,1)}, bf16[512,512]{1,0:T(8,128)(2,1)S(1)}, u32[]{:S(2)}, u32[]{:S(2)}) %collective-permute-start.37) | collective-permute-done | bytes 524320 | tf_op jit(solution)/shard_map/ppermute | solution.py:384
  341.3 4.9 %shard_map.69 = (bf16[512,1792]{1,0:T(8,128)(2,1)}, bf16[512,1792]{1,0:T(8,128)(2,1)}) custom-call(s32[1]{0:T(128)} %bitcast.meta_ref, bf16[512,384]{1,0:T(8,128)(2,1)} %get-tuple-element.77.refs_0_, bf16[512,384]{1,0:T(8,128)(2,1)} %copy-done.23, bf16[512,384]{1,0:T(8,128)(2,1)} %copy-done.24, bf16[512,384]{1,0:T(8,128)(2,1)} %copy-done.25, ...), custom_call_target="tpu_custom_call" | custom-call | flops 1 | bytes 1 | tf_op jit(solution)/shard_map/pallas_call | solution.py:356
  (142 shorter events, 57.0 us)
Async XLA Ops:
  7.2 25.7 %collective-permute-start.1 = (bf16[256,512]{1,0:T(8,128)(2,1)}, bf16[256,512]{1,0:T(8,128)(2,1)S(1)}, u32[]{:S(2)}, u32[]{:S(2)}) collective-permute-start(bf16[256,512]{1,0:T(8,128)(2,1)} %param.6), channel_id=1, source_target_pairs={{0,64},{16,80},{32,96},{48,112},{64,0},{80,16},{96,32},{112,48},{1... | collective-permute-start | bytes 786440 | tf_op jit(solution)/shard_map/ppermute | solution.py:389
  11.0 21.8 %collective-permute-start = (bf16[256,512]{1,0:T(8,128)(2,1)}, bf16[256,512]{1,0:T(8,128)(2,1)S(1)}, u32[]{:S(2)}, u32[]{:S(2)}) collective-permute-start(bf16[256,512]{1,0:T(8,128)(2,1)} %param.6), channel_id=1, source_target_pairs={{0,32},{16,48},{32,64},{48,80},{64,96},{80,112},{96,0},{112,16},{1... | collective-permute-start | bytes 786440 | tf_op jit(solution)/shard_map/ppermute | solution.py:389
  11.4 21.4 %collective-permute-start.2 = (bf16[256,512]{1,0:T(8,128)(2,1)}, bf16[256,512]{1,0:T(8,128)(2,1)S(1)}, u32[]{:S(2)}, u32[]{:S(2)}) collective-permute-start(bf16[256,512]{1,0:T(8,128)(2,1)} %param.6), channel_id=1, source_target_pairs={{0,96},{16,112},{32,0},{48,16},{64,32},{80,48},{96,64},{112,80},{1... | collective-permute-start | bytes 786440 | tf_op jit(solution)/shard_map/ppermute | solution.py:389
  33.0 62.1 %all-to-all-start = ((bf16[8,352,768]{2,1,0:T(8,128)(2,1)}), bf16[8,352,768]{2,1,0:T(8,128)(2,1)}, u32[]{:S(2)}, u32[]{:S(2)}) async-start(bf16[8,352,768]{2,1,0:T(8,128)(2,1)} %shard_map.59), calls=%async_computation | async-start | bytes 8650752 | tf_op jit(solution)/shard_map/all_to_all | solution.py:405
  38.6 56.4 %collective-permute-start.6 = (bf16[4,256,512]{2,1,0:T(8,128)(2,1)S(1)}, bf16[4,256,512]{2,1,0:T(8,128)(2,1)S(1)}, u32[]{:S(2)}, u32[]{:S(2)}) collective-permute-start(bf16[4,256,512]{2,1,0:T(8,128)(2,1)S(1)} %pad_maximum_fusion.refs_0_), channel_id=1, source_target_pairs={{0,3},{1,0},{2,1},{3,2},{4,7},{5,4},{6,5},{7,6},{8,11},{9,8},{10,9... | collective-permute-start | bytes 3145736 | tf_op jit(solution)/shard_map/ppermute | solution.py:384
  40.5 54.6 %collective-permute-start.5 = (bf16[4,256,512]{2,1,0:T(8,128)(2,1)S(1)}, bf16[4,256,512]{2,1,0:T(8,128)(2,1)S(1)}, u32[]{:S(2)}, u32[]{:S(2)}) collective-permute-start(bf16[4,256,512]{2,1,0:T(8,128)(2,1)S(1)} %pad_maximum_fusion.refs_0_), channel_id=1, source_target_pairs={{0,2},{1,3},{2,0},{3,1},{4,6},{5,7},{6,4},{7,5},{8,10},{9,11},{10,... | collective-permute-start | bytes 3145736 | tf_op jit(solution)/shard_map/ppermute | solution.py:384
  41.3 53.8 %collective-permute-start.4 = (bf16[4,256,512]{2,1,0:T(8,128)(2,1)S(1)}, bf16[4,256,512]{2,1,0:T(8,128)(2,1)}, u32[]{:S(2)}, u32[]{:S(2)}) collective-permute-start(bf16[4,256,512]{2,1,0:T(8,128)(2,1)S(1)} %pad_maximum_fusion.refs_0_), channel_id=1, source_target_pairs={{0,1},{1,2},{2,3},{3,0},{4,5},{5,6},{6,7},{7,4},{8,9},{9,10},{10,1... | collective-permute-start | bytes 3145736 | tf_op jit(solution)/shard_map/ppermute | solution.py:384
  56.5 33.0 %collective-permute-start.9 = (bf16[256,384]{1,0:T(8,128)(2,1)S(1)}, bf16[256,384]{1,0:T(8,128)(2,1)S(1)}, u32[]{:S(2)}, u32[]{:S(2)}) collective-permute-start(bf16[256,384]{1,0:T(8,128)(2,1)S(1)} %collective-permute-done.3), channel_id=1, source_target_pairs={{0,3},{4,7},{8,11},{12,15},{16,19},{20,23},{24,27},{28,31},{32,35}... | collective-permute-start | bytes 589832 | tf_op jit(solution)/shard_map/ppermute | solution.py:416
  60.0 30.8 %collective-permute-start.8 = (bf16[256,384]{1,0:T(8,128)(2,1)S(1)}, bf16[256,384]{1,0:T(8,128)(2,1)S(1)}, u32[]{:S(2)}, u32[]{:S(2)}) collective-permute-start(bf16[256,384]{1,0:T(8,128)(2,1)S(1)} %collective-permute-done.3), channel_id=1, source_target_pairs={{0,2},{4,6},{8,10},{12,14},{16,18},{20,22},{24,26},{28,30},{32,34}... | collective-permute-start | bytes 589832 | tf_op jit(solution)/shard_map/ppermute | solution.py:416
  95.1 78.3 %all-to-all-start.1 = ((bf16[8,352,1024]{2,1,0:T(8,128)(2,1)}), bf16[8,352,1024]{2,1,0:T(8,128)(2,1)}, u32[]{:S(2)}, u32[]{:S(2)}) async-start(bf16[8,352,1024]{2,1,0:T(8,128)(2,1)} %shard_map.60), calls=%async_computation.1 | async-start | bytes 11534336 | tf_op jit(solution)/shard_map/all_to_all | solution.py:405
  101.3 48.9 %all-gather.6.cloned.1.call-start = ((), (), s32[]{:S(2)}) async-start(), calls=%async_computation.3 | async-start | bytes 1769472 | tf_op jit(solution)/shard_map/all_gather | solution.py:467
  102.0 103.8 %all-gather.4.cloned.1.call-start = ((), (), s32[]{:S(2)}) async-start(), calls=%async_computation.2 | async-start | bytes 2293760 | tf_op jit(solution)/shard_map/all_gather | solution.py:485
  115.9 33.1 %collective-permute-start.14 = (bf16[896,384]{1,0:T(8,128)(2,1)}, bf16[896,384]{1,0:T(8,128)(2,1)S(1)}, u32[]{:S(2)}, u32[]{:S(2)}) collective-permute-start(bf16[896,384]{1,0:T(8,128)(2,1)} %get-tuple-element.59), channel_id=1, source_target_pairs={{0,1},{1,2},{2,3},{3,0},{4,5},{5,6},{6,7},{7,4},{8,9},{9,10},{10,1... | collective-permute-start | bytes 2064392 | tf_op jit(solution)/shard_map/ppermute | solution.py:384
  118.2 30.9 %collective-permute-start.15 = (bf16[896,384]{1,0:T(8,128)(2,1)}, bf16[896,384]{1,0:T(8,128)(2,1)S(1)}, u32[]{:S(2)}, u32[]{:S(2)}) collective-permute-start(bf16[896,384]{1,0:T(8,128)(2,1)} %get-tuple-element.60), channel_id=1, source_target_pairs={{0,2},{1,3},{2,0},{3,1},{4,6},{5,7},{6,4},{7,5},{8,10},{9,11},{10,... | collective-permute-start | bytes 2064392 | tf_op jit(solution)/shard_map/ppermute | solution.py:384
  118.2 31.2 %collective-permute-start.16 = (bf16[896,384]{1,0:T(8,128)(2,1)}, bf16[896,384]{1,0:T(8,128)(2,1)S(1)}, u32[]{:S(2)}, u32[]{:S(2)}) collective-permute-start(bf16[896,384]{1,0:T(8,128)(2,1)} %get-tuple-element.61), channel_id=1, source_target_pairs={{0,3},{1,0},{2,1},{3,2},{4,7},{5,4},{6,5},{7,6},{8,11},{9,8},{10,9... | collective-permute-start | bytes 2064392 | tf_op jit(solution)/shard_map/ppermute | solution.py:384
  163.0 25.2 %collective-permute-start.17 = (bf16[512,384]{1,0:T(8,128)(2,1)}, bf16[512,384]{1,0:T(8,128)(2,1)S(1)}, u32[]{:S(2)}, u32[]{:S(2)}) collective-permute-start(bf16[512,384]{1,0:T(8,128)(2,1)} %get-tuple-element.67), channel_id=1, source_target_pairs={{0,4},{1,5},{2,6},{3,7},{4,8},{5,9},{6,10},{7,11},{8,12},{9,13},{1... | collective-permute-start | bytes 1179656 | tf_op jit(solution)/shard_map/ppermute | solution.py:377
  179.9 42.1 %collective-permute-start.20 = (bf16[896,512]{1,0:T(8,128)(2,1)}, bf16[896,512]{1,0:T(8,128)(2,1)S(1)}, u32[]{:S(2)}, u32[]{:S(2)}) collective-permute-start(bf16[896,512]{1,0:T(8,128)(2,1)} %get-tuple-element.72), channel_id=1, source_target_pairs={{0,1},{1,2},{2,3},{3,0},{4,5},{5,6},{6,7},{7,4},{8,9},{9,10},{10,1... | collective-permute-start | bytes 2752520 | tf_op jit(solution)/shard_map/ppermute | solution.py:384
  182.1 41.7 %collective-permute-start.21 = (bf16[896,512]{1,0:T(8,128)(2,1)}, bf16[896,512]{1,0:T(8,128)(2,1)S(1)}, u32[]{:S(2)}, u32[]{:S(2)}) collective-permute-start(bf16[896,512]{1,0:T(8,128)(2,1)} %get-tuple-element.73), channel_id=1, source_target_pairs={{0,2},{1,3},{2,0},{3,1},{4,6},{5,7},{6,4},{7,5},{8,10},{9,11},{10,... | collective-permute-start | bytes 2752520 | tf_op jit(solution)/shard_map/ppermute | solution.py:384
  182.1 41.7 %collective-permute-start.22 = (bf16[896,512]{1,0:T(8,128)(2,1)}, bf16[896,512]{1,0:T(8,128)(2,1)S(1)}, u32[]{:S(2)}, u32[]{:S(2)}) collective-permute-start(bf16[896,512]{1,0:T(8,128)(2,1)} %get-tuple-element.74), channel_id=1, source_target_pairs={{0,3},{1,0},{2,1},{3,2},{4,7},{5,4},{6,5},{7,6},{8,11},{9,8},{10,9... | collective-permute-start | bytes 2752520 | tf_op jit(solution)/shard_map/ppermute | solution.py:384
  209.6 33.3 %collective-permute-start.25 = (bf16[512,384]{1,0:T(8,128)(2,1)}, bf16[512,384]{1,0:T(8,128)(2,1)S(1)}, u32[]{:S(2)}, u32[]{:S(2)}) collective-permute-start(bf16[512,384]{1,0:T(8,128)(2,1)} %shard_map.64.refs_8_), channel_id=1, source_target_pairs={{0,12},{1,13},{2,14},{3,15},{4,0},{5,1},{6,2},{7,3},{8,4},{9,5},{1... | collective-permute-start | bytes 1179656 | tf_op jit(solution)/shard_map/ppermute | solution.py:377
  212.9 32.3 %collective-permute-start.24 = (bf16[512,384]{1,0:T(8,128)(2,1)}, bf16[512,384]{1,0:T(8,128)(2,1)S(1)}, u32[]{:S(2)}, u32[]{:S(2)}) collective-permute-start(bf16[512,384]{1,0:T(8,128)(2,1)} %shard_map.64.refs_8_), channel_id=1, source_target_pairs={{0,8},{1,9},{2,10},{3,11},{4,12},{5,13},{6,14},{7,15},{8,0},{9,1},... | collective-permute-start | bytes 1179656 | tf_op jit(solution)/shard_map/ppermute | solution.py:377
  222.0 23.2 %collective-permute-start.23 = (bf16[512,384]{1,0:T(8,128)(2,1)}, bf16[512,384]{1,0:T(8,128)(2,1)}, u32[]{:S(2)}, u32[]{:S(2)}) collective-permute-start(bf16[512,384]{1,0:T(8,128)(2,1)} %shard_map.64.refs_8_), channel_id=1, source_target_pairs={{0,4},{1,5},{2,6},{3,7},{4,8},{5,9},{6,10},{7,11},{8,12},{9,13},{1... | collective-permute-start | bytes 1179656 | tf_op jit(solution)/shard_map/ppermute | solution.py:377
  240.6 23.9 %collective-permute-start.30 = (bf16[512,512]{1,0:T(8,128)(2,1)}, bf16[512,512]{1,0:T(8,128)(2,1)S(1)}, u32[]{:S(2)}, u32[]{:S(2)}) collective-permute-start(bf16[512,512]{1,0:T(8,128)(2,1)} %get-tuple-element.83), channel_id=1, source_target_pairs={{0,8},{1,9},{2,10},{3,11},{4,12},{5,13},{6,14},{7,15},{8,0},{9,1},... | collective-permute-start | bytes 1572872 | tf_op jit(solution)/shard_map/ppermute | solution.py:377
  242.9 22.4 %collective-permute-start.31 = (bf16[512,512]{1,0:T(8,128)(2,1)}, bf16[512,512]{1,0:T(8,128)(2,1)S(1)}, u32[]{:S(2)}, u32[]{:S(2)}) collective-permute-start(bf16[512,512]{1,0:T(8,128)(2,1)} %get-tuple-element.84), channel_id=1, source_target_pairs={{0,12},{1,13},{2,14},{3,15},{4,0},{5,1},{6,2},{7,3},{8,4},{9,5},{1... | collective-permute-start | bytes 1572872 | tf_op jit(solution)/shard_map/ppermute | solution.py:377
  254.6 21.6 %collective-permute-start.26 = (bf16[512,384]{1,0:T(8,128)(2,1)}, bf16[512,384]{1,0:T(8,128)(2,1)S(1)}, u32[]{:S(2)}, u32[]{:S(2)}) collective-permute-start(bf16[512,384]{1,0:T(8,128)(2,1)} %get-tuple-element.78), channel_id=1, source_target_pairs={{0,3},{1,0},{2,1},{3,2},{4,7},{5,4},{6,5},{7,6},{8,11},{9,8},{10,9... | collective-permute-start | bytes 1179656 | tf_op jit(solution)/shard_map/ppermute | solution.py:384
  269.9 25.5 %collective-permute-start.34 = (bf16[512,512]{1,0:T(8,128)(2,1)}, bf16[512,512]{1,0:T(8,128)(2,1)S(1)}, u32[]{:S(2)}, u32[]{:S(2)}) collective-permute-start(bf16[512,512]{1,0:T(8,128)(2,1)} %shard_map.67.refs_8_), channel_id=1, source_target_pairs={{0,12},{1,13},{2,14},{3,15},{4,0},{5,1},{6,2},{7,3},{8,4},{9,5},{1... | collective-permute-start | bytes 1572872 | tf_op jit(solution)/shard_map/ppermute | solution.py:377
  273.2 22.2 %collective-permute-start.33 = (bf16[512,512]{1,0:T(8,128)(2,1)}, bf16[512,512]{1,0:T(8,128)(2,1)S(1)}, u32[]{:S(2)}, u32[]{:S(2)}) collective-permute-start(bf16[512,512]{1,0:T(8,128)(2,1)} %shard_map.67.refs_8_), channel_id=1, source_target_pairs={{0,8},{1,9},{2,10},{3,11},{4,12},{5,13},{6,14},{7,15},{8,0},{9,1},... | collective-permute-start | bytes 1572872 | tf_op jit(solution)/shard_map/ppermute | solution.py:377
  273.2 26.1 %collective-permute-start.32 = (bf16[512,512]{1,0:T(8,128)(2,1)}, bf16[512,512]{1,0:T(8,128)(2,1)S(1)}, u32[]{:S(2)}, u32[]{:S(2)}) collective-permute-start(bf16[512,512]{1,0:T(8,128)(2,1)} %shard_map.67.refs_8_), channel_id=1, source_target_pairs={{0,4},{1,5},{2,6},{3,7},{4,8},{5,9},{6,10},{7,11},{8,12},{9,13},{1... | collective-permute-start | bytes 1572872 | tf_op jit(solution)/shard_map/ppermute | solution.py:377
  276.2 18.5 %collective-permute-start.28 = (bf16[512,384]{1,0:T(8,128)(2,1)S(1)}, bf16[512,384]{1,0:T(8,128)(2,1)S(1)}, u32[]{:S(2)}, u32[]{:S(2)}) collective-permute-start(bf16[512,384]{1,0:T(8,128)(2,1)S(1)} %copy-done.26), channel_id=1, source_target_pairs={{0,1},{1,2},{2,3},{3,0},{4,5},{5,6},{6,7},{7,4},{8,9},{9,10},{10,1... | collective-permute-start | bytes 1179656 | tf_op jit(solution)/shard_map/ppermute | solution.py:384
  310.0 25.8 %collective-permute-start.35 = (bf16[512,512]{1,0:T(8,128)(2,1)}, bf16[512,512]{1,0:T(8,128)(2,1)S(1)}, u32[]{:S(2)}, u32[]{:S(2)}) collective-permute-start(bf16[512,512]{1,0:T(8,128)(2,1)} %get-tuple-element.87), channel_id=1, source_target_pairs={{0,3},{1,0},{2,1},{3,2},{4,7},{5,4},{6,5},{7,6},{8,11},{9,8},{10,9... | collective-permute-start | bytes 1572872 | tf_op jit(solution)/shard_map/ppermute | solution.py:384
  313.7 22.2 %collective-permute-start.36 = (bf16[512,512]{1,0:T(8,128)(2,1)}, bf16[512,512]{1,0:T(8,128)(2,1)S(1)}, u32[]{:S(2)}, u32[]{:S(2)}) collective-permute-start(bf16[512,512]{1,0:T(8,128)(2,1)} %get-tuple-element.88), channel_id=1, source_target_pairs={{0,2},{1,3},{2,0},{3,1},{4,6},{5,7},{6,4},{7,5},{8,10},{9,11},{10,... | collective-permute-start | bytes 1572872 | tf_op jit(solution)/shard_map/ppermute | solution.py:384
  314.3 26.1 %collective-permute-start.37 = (bf16[512,512]{1,0:T(8,128)(2,1)}, bf16[512,512]{1,0:T(8,128)(2,1)S(1)}, u32[]{:S(2)}, u32[]{:S(2)}) collective-permute-start(bf16[512,512]{1,0:T(8,128)(2,1)} %get-tuple-element.89), channel_id=1, source_target_pairs={{0,1},{1,2},{2,3},{3,0},{4,5},{5,6},{6,7},{7,4},{8,9},{9,10},{10,1... | collective-permute-start | bytes 1572872 | tf_op jit(solution)/shard_map/ppermute | solution.py:384
  (39 other events, 488.6 us)
Sparse Core Ops, SparseCore 0:
  103.8 30.6 all-gather.5
  149.5 31.8 all-gather.3
